TPU v7x, 512 devices: a whole 4x4x16 slice. The times are simulated.
512 devices in a mesh: row: 32 (over x_lo, z), col: 16 (over y, x_hi, core).
Axes of the slice: x: 4 (x_hi: 2, x_lo: 2; x = x_hi * 2 + x_lo), y: 4, z: 16, core: 2. Of those that a mesh axis runs over, the one named last changes fastest.
Arguments:
- matrix: float32 [16384, 16384], P('row', 'col'), may hold values from -10 to 10, as said below
- vectors: float32 [2, 16384, 128], P(None, ('row', 'col')), may hold values from -0.09375 to 0.09375
- factors: float32 [2, 128, 128], replicated, may hold values from -0.5 to 1.5, as said below
Outputs:
- updated: float32 [16384, 16384], P('row', 'col')
Inputs may be any that keep to these rules, and one draw needn't show every extreme that they name: matrix is exactly symmetric. Each factors[p] is upper triangular with a positive diagonal.
All inputs are finite; a program needn't handle non-finite values.
Results may differ from a plain program's by a relative error of at most 0.00013.
Values sent between devices are 32-bit elements; how exact they have to be, the bound alone decides.
No kernel may reach another device: no remote copies, remote signals or barrier semaphores. Data moves between devices by JAX's collectives and lax.ppermute only.
A program may use at most 64 MiB of HBM per device.

v0:
```python
import jax
import jax.numpy as jnp
from jax import lax
from jax.sharding import PartitionSpec as P

HIGH = lax.Precision.HIGHEST


def broadcast(value, axis, source):
    kept = jnp.where(lax.axis_index(axis) == source, value, 0).astype(value.dtype)
    return lax.psum(kept, axis)


def matmul(left, right):
    return jnp.dot(left, right, precision=HIGH, preferred_element_type=jnp.float32)


def contract_first(left, right):
    return lax.dot_general(
        left, right, (((0,), (0,)), ((), ())), precision=HIGH, preferred_element_type=jnp.float32
    )


def contract_last(left, right):
    return lax.dot_general(
        left, right, (((1,), (1,)), ((), ())), precision=HIGH, preferred_element_type=jnp.float32
    )


def body(matrix, vectors, factors):
    ratio = lax.axis_size("row") // lax.axis_size("col")
    col_place = lax.axis_index("col")
    all_rows = lax.all_gather(vectors, "col", axis=1, tiled=True)
    col_parts = [broadcast(all_rows, "row", col_place * ratio + offset) for offset in range(ratio)]
    all_cols = jnp.concatenate(col_parts, axis=1)
    panels = vectors.shape[0]
    current = matrix
    for panel in range(panels):
        basis_rows = all_rows[panel]
        basis_cols = all_cols[panel]
        factor = factors[panel]
        prod = lax.psum(matmul(current, basis_cols), "col")
        xmat = matmul(prod, factor)
        proj = lax.psum(contract_first(basis_rows, xmat), "row")
        w_block = xmat - 0.5 * matmul(basis_rows, contract_first(factor, proj))
        w_parts = [broadcast(w_block, "row", col_place * ratio + offset) for offset in range(ratio)]
        w_column = jnp.concatenate(w_parts, axis=0)
        current = current - contract_last(basis_rows, w_column) - contract_last(w_block, basis_cols)
    return current


def solution(mesh):
    in_specs = (P("row", "col"), P(None, ("row", "col"), None), P())
    out_specs = P("row", "col")
    return jax.shard_map(body, mesh=mesh, in_specs=in_specs, out_specs=out_specs, check_vma=False)
```

profile of v0, /device:TPU:1, one launch (start us, length us, event | category | flops | bytes accessed | tf_op | source)
XLA Modules:
  0.0 1596.4 jit_solution(3622642844782837041)
XLA Ops:
  6.5 0.0 all-reduce.23.cloned.1.call-start
  6.5 29.0 %all_gather.3 = f32[2,512,128]{2,1,0:T(8,128)S(1)} all-gather(f32[2,32,128]{2,1,0:T(8,128)} %param.4), channel_id=1, replica_groups=mesh['row'=32,'col'=16] {'col'}, dimensions={1}, use_global_device_ids=true | all-gather | bytes 557056 | tf_op jit(solution)/shard_map/all_gather | solution.py:33
  35.5 1.1 broadcast_select_fusion
  36.6 0.0 all-reduce.23.cloned.1.call-update
  36.6 0.0 all-reduce.11.cloned.1.call-start
  36.7 235.7 %all-reduce.23.cloned.1.call-done = (f32[2,512,128]{2,1,0:T(8,128)}, f32[2,512,128]{2,1,0:T(8,128)}) async-done(((f32[2,512,128]{2,1,0:T(8,128)}, f32[2,512,128]{2,1,0:T(8,128)}), (f32[2,512,128]{2,1,0:T(8,128)}, f32[2,512,128]{2,1,0:T(8,128)})) %all-reduce.23.cloned.1.call-update) | async-done | bytes 1048592 | tf_op jit(solution)/shard_map/psum | solution.py:11
  272.4 1.1 constant_dynamic-update-slice_fusion.1
  273.4 0.0 copy-start.5
  273.4 1.1 constant_dynamic-update-slice_fusion
  274.6 0.0 copy-start.2
  274.6 1.0 copy-done.2
  275.5 0.0 copy-done.1
  275.5 3.0 convolution_bitcast_fusion
  278.6 0.0 all-reduce.11.cloned.1.call-update
  278.6 0.0 all-reduce.13.cloned.1.call-start
  278.7 167.4 %all-reduce.11.cloned.1.call-done = f32[512,128]{0,1:T(8,128)} async-done(((f32[512,128]{0,1:T(8,128)}), f32[512,128]{0,1:T(8,128)}) %all-reduce.11.cloned.1.call-update) | async-done | bytes 262160 | tf_op jit(solution)/shard_map/psum | solution.py:42
  446.1 0.0 copy-done.5
  446.1 1.5 fusion.21
  447.6 1.2 convolution_bitcast_fusion.2
  448.9 0.0 all-reduce.13.cloned.1.call-update
  448.9 0.0 all-reduce.21.cloned.1.call-start
  448.9 216.8 %all-reduce.13.cloned.1.call-done = f32[128,128]{0,1:T(8,128)} async-done(((f32[128,128]{0,1:T(8,128)}), f32[128,128]{0,1:T(8,128)}) %all-reduce.13.cloned.1.call-update) | async-done | bytes 65552 | tf_op jit(solution)/shard_map/psum | solution.py:44
  665.8 1.0 fusion.19
  666.8 1.2 broadcast_select_fusion.5
  668.0 0.0 all-reduce.21.cloned.1.call-update
  668.0 0.0 all-reduce.15.cloned.1.call-start
  668.1 1.8 copy.5
  669.9 254.5 %all-reduce.21.cloned.1.call-done = (f32[512,128]{1,0:T(8,128)}, f32[512,128]{1,0:T(8,128)}) async-done(((f32[512,128]{1,0:T(8,128)}, f32[512,128]{1,0:T(8,128)}), (f32[512,128]{1,0:T(8,128)}, f32[512,128]{1,0:T(8,128)})) %all-reduce.21.cloned.1.call-update) | async-done | bytes 524304 | tf_op jit(solution)/shard_map/psum | solution.py:11
  924.4 3.0 fusion.6
  927.4 0.0 copy-done
  927.4 0.0 copy-start.3
  927.4 3.1 fusion.1
  930.6 4.1 fusion.14
  934.7 0.0 all-reduce.15.cloned.1.call-update
  934.7 0.2 all-reduce.17.cloned.1.call-start
  935.0 167.2 %all-reduce.15.cloned.1.call-done = f32[512,128]{1,0:T(8,128)} async-done(((f32[512,128]{1,0:T(8,128)}), f32[512,128]{1,0:T(8,128)}) %all-reduce.15.cloned.1.call-update) | async-done | bytes 262160 | tf_op jit(solution)/shard_map/psum | solution.py:42
  1102.1 1.3 fusion.17
  1103.5 1.2 convolution_bitcast_fusion.1
  1104.7 0.0 all-reduce.17.cloned.1.call-update
  1104.7 0.0 all-reduce.19.cloned.1.call-start
  1104.7 217.2 %all-reduce.17.cloned.1.call-done = f32[128,128]{0,1:T(8,128)} async-done(((f32[128,128]{0,1:T(8,128)}), f32[128,128]{0,1:T(8,128)}) %all-reduce.17.cloned.1.call-update) | async-done | bytes 65552 | tf_op jit(solution)/shard_map/psum | solution.py:44
  1321.9 1.0 fusion.15
  1323.0 1.2 broadcast_select_fusion.3
  1324.2 0.0 all-reduce.19.cloned.1.call-update
  1324.2 256.2 %all-reduce.19.cloned.1.call-done = (f32[512,128]{1,0:T(8,128)}, f32[512,128]{1,0:T(8,128)}) async-done(((f32[512,128]{1,0:T(8,128)}, f32[512,128]{1,0:T(8,128)}), (f32[512,128]{1,0:T(8,128)}, f32[512,128]{1,0:T(8,128)})) %all-reduce.19.cloned.1.call-update) | async-done | bytes 524304 | tf_op jit(solution)/shard_map/psum | solution.py:11
  1580.4 2.9 fusion.10
  1583.3 3.4 fusion
  1586.7 2.9 copy.9
  (5 shorter events, 0.0 us)
Async XLA Ops:
  6.5 265.8 %all-reduce.23.cloned.1.call-start = ((), (), s32[]{:S(2)}) async-start(), calls=%async_computation.6 | async-start | bytes 2097152 | tf_op jit(solution)/shard_map/psum | solution.py:11
  35.5 240.0 %copy-start.1 = (f32[512,1024]{1,0:T(8,128)S(1)}, f32[512,1024]{1,0:T(8,128)}, u32[]{:S(2)}) copy-start(f32[512,1024]{1,0:T(8,128)} %param.3) | copy-start | bytes 6291460
  36.6 409.5 %all-reduce.11.cloned.1.call-start = ((), (), s32[]{:S(2)}) async-start(), calls=%async_computation | async-start | bytes 524288 | tf_op jit(solution)/shard_map/psum | solution.py:42
  273.4 172.7 %copy-start.5 = (f32[2,128,128]{2,1,0:T(8,128)S(1)}, f32[2,128,128]{2,1,0:T(8,128)}, u32[]{:S(2)}) copy-start(f32[2,128,128]{2,1,0:T(8,128)} %param.5) | copy-start | bytes 393220
  274.6 1.0 copy-start.2
  278.6 387.2 %all-reduce.13.cloned.1.call-start = ((), (), s32[]{:S(2)}) async-start(), calls=%async_computation.1 | async-start | bytes 131072 | tf_op jit(solution)/shard_map/psum | solution.py:44
  448.9 475.5 %all-reduce.21.cloned.1.call-start = ((), (), s32[]{:S(2)}) async-start(), calls=%async_computation.5 | async-start | bytes 1048576 | tf_op jit(solution)/shard_map/psum | solution.py:11
  668.0 434.1 %all-reduce.15.cloned.1.call-start = ((), (), s32[]{:S(2)}) async-start(), calls=%async_computation.2 | async-start | bytes 524288 | tf_op jit(solution)/shard_map/psum | solution.py:42
  924.4 3.0 copy-start
  927.4 3.2 copy-start.3
  934.7 387.2 %all-reduce.17.cloned.1.call-start = ((), (), s32[]{:S(2)}) async-start(), calls=%async_computation.3 | async-start | bytes 131072 | tf_op jit(solution)/shard_map/psum | solution.py:44
  1104.7 475.7 %all-reduce.19.cloned.1.call-start = ((), (), s32[]{:S(2)}) async-start(), calls=%async_computation.4 | async-start | bytes 1048576 | tf_op jit(solution)/shard_map/psum | solution.py:11
  1580.4 2.9 copy-start.4
Sparse Core Ops, SparseCore 0:
  36.7 235.5 all-reduce.22
  278.7 167.3 all-reduce.10
  449.0 216.7 all-reduce.12
  668.8 255.5 all-reduce.20
  934.8 167.2 all-reduce.14
  1105.2 216.7 all-reduce.16
  1324.9 255.4 all-reduce.18
where the time goes:
time: 1620 us; the launch traced here: 1600 us
  waiting for transfers between devices  1520 us (94%)
  matrix products  29.3 us (2%)
  blocking collectives  29 us (2%)
    psum x3, waiting for transfers between devices, broadcast(): return lax.psum(kept, axis)  746 us
    psum x2, waiting for transfers between devices, body(): proj = lax.psum(contract_first(basis_rows, xmat), 'row')  434 us
    psum x2, waiting for transfers between devices, body(): prod = lax.psum(matmul(current, basis_cols), 'col')  335 us
  transfers between devices with their start and end apart: 7, of which 7 were waited for; matrix products, arithmetic and copies ran while one was open for 0% of the time, Pallas kernels for 0%

commit v1 on v0

v1 whole, which is shorter than its diff:
```python
import jax
import jax.numpy as jnp
from jax import lax
from jax.sharding import Mesh, PartitionSpec as P

HIGH = lax.Precision.HIGH
HIGHEST = lax.Precision.HIGHEST
DEPTH = "z"
PLANE = ("y", "x_hi", "core", "x_lo")


def matmul(left, right, precision=HIGH):
    return jnp.dot(left, right, precision=precision, preferred_element_type=jnp.float32)


def contract_first(left, right, precision=HIGH):
    return lax.dot_general(
        left, right, (((0,), (0,)), ((), ())), precision=precision, preferred_element_type=jnp.float32
    )


def contract_last(left, right, precision=HIGH):
    return lax.dot_general(
        left, right, (((1,), (1,)), ((), ())), precision=precision, preferred_element_type=jnp.float32
    )


def exchange(parts, axes):
    return lax.all_to_all(parts, axes, 0, 0)


def spread(stack, own, extra=None):
    width = stack.shape[-1]
    cols = stack.reshape(8, 2, 2, 16, width).transpose(2, 0, 1, 3, 4).reshape(16, 1, 32, width)
    pieces = [jnp.broadcast_to(cols, (16, 2, 32, width)), jnp.broadcast_to(own[None], (16, 2, 16, width))]
    if extra is not None:
        pieces.append(jnp.broadcast_to(extra[None, None], (16, 2) + extra.shape))
    message = jnp.concatenate(pieces, axis=2)
    message = message.reshape((32,) + message.shape[2:])
    got = exchange(message, PLANE)
    col_rows = jnp.concatenate([got[:, :16].reshape(512, width), got[:, 16:32].reshape(512, width)], axis=0)
    row_rows = got[:, 32:48].reshape(512, width)
    if extra is None:
        return col_rows, row_rows
    return col_rows, row_rows, got[:, 48:].reshape(-1, width)


def coefficients(gram, factors):
    k = factors.shape[-1]
    f1, f2 = factors[0], factors[1]
    g11, g12, h12, g22 = gram[:k, :k], gram[:k, k:], gram[k:, :k], gram[k:, k:]
    mm = lambda a, b: matmul(a, b, HIGHEST)
    mt = lambda a, b: contract_first(a, b, HIGHEST)
    b1 = -0.5 * mt(f1, mm(g11, f1))
    m = mt(f1, g12) + mt(b1, h12)
    fh = mm(f1, h12)
    c = m + mm(b1, h12)
    s2 = mm(g22 - mt(g12, fh) - mt(h12, c), f2)
    b2 = -0.5 * mt(f2, s2)
    zero = jnp.zeros_like(f1)
    p = jnp.block([[f1, -mm(fh, f2)], [zero, f2]])
    q = jnp.block([[b1, -mm(c, f2)], [zero, b2]])
    return p, q


def body(matrix, vectors, factors):
    k = vectors.shape[-1]
    mine = jnp.concatenate([vectors[0], vectors[1]], axis=1)
    own_v = exchange(mine.reshape(2, 16, 2 * k), "x_lo")
    all_v = lax.all_gather(own_v, DEPTH)
    v_col, v_row = spread(all_v, own_v)
    part = matmul(matrix, v_col)
    gram = contract_first(v_row, part)
    flat = own_v.reshape(32, 2 * k)
    cross = contract_first(flat[:, :k], flat[:, k:])
    gram = jnp.concatenate([gram[:k], jnp.concatenate([cross, gram[k:, k:]], axis=1)], axis=0)
    sums = exchange(
        jnp.concatenate([part.reshape(32, 16, 2 * k), gram.reshape(32, 8, 2 * k)], axis=1), PLANE
    ).reshape(16, 2, 24, 2 * k)
    sums = jnp.sum(sums, axis=0)
    own_z = sums[:, :16]
    own_g = jnp.sum(sums[:, 16:], axis=0)
    gathered = lax.all_gather(jnp.concatenate([own_z.reshape(32, 2 * k), own_g], axis=0), DEPTH)
    all_z = gathered[:, :32].reshape(16, 2, 16, 2 * k)
    piece = jnp.sum(gathered[:, 32:], axis=0)
    z_col, z_row, gram = spread(all_z, own_z, piece)
    p, q = coefficients(gram, factors)
    left = jnp.concatenate([contract_last(v_row, p), matmul(z_row, p) + matmul(v_row, q + q.T)], axis=1)
    right = jnp.concatenate([z_col, v_col], axis=1)
    return matrix - contract_last(left, right)


def solution(mesh):
    fine = Mesh(mesh.devices.reshape(2, 16, 4, 2, 2), ("x_lo", "z", "y", "x_hi", "core"))
    row, col = ("x_lo", "z"), ("y", "x_hi", "core")
    in_specs = (P(row, col), P(None, row + col, None), P())
    return jax.shard_map(body, mesh=fine, in_specs=in_specs, out_specs=P(row, col), check_vma=False)
```

time: 1620 us -> 188 us (0.12); the launches traced: 1600 us -> 186 us
  waiting for transfers between devices: 1520 us -> 44.6 us
  blocking collectives: 29 us -> 80.9 us
  starting transfers between devices: 0.43 us -> 27.9 us
    psum x7 -> x0, waiting for transfers between devices: 1520 us -> none  [the longest x3 746 us: broadcast(): return lax.psum(kept, axis)]
    all_to_all x0 -> x2, waiting for transfers between devices: none -> 44.6 us  [exchange(): return lax.all_to_all(parts, axes, 0, 0)]
    all_to_all x0 -> x2, starting transfers between devices: none -> 27.9 us  [exchange(): return lax.all_to_all(parts, axes, 0, 0)]
    all_gather x1 -> x2, blocking collectives: 29 us -> 55.2 us  [the longest x1 32 us: body(): all_v = lax.all_gather(own_v, DEPTH)]
    all_to_all x0 -> x2, blocking collectives: none -> 25.7 us  [exchange(): return lax.all_to_all(parts, axes, 0, 0)]
  transfers between devices with their start and end apart: 7 -> 2, of which waited for: 7 -> 2; matrix products, arithmetic and copies ran while one was open for 0% -> 0% of each run, Pallas kernels for 0% -> 0%
where the time goes in v1:
time: 188 us; the launch traced here: 186 us
  blocking collectives  80.9 us (43%)
  waiting for transfers between devices  44.6 us (24%)
  starting transfers between devices  27.9 us (15%)
  matrix products  16.1 us (9%)
  local copies, waits for them, and re-layouts  10.3 us (5%)
  other arithmetic  5.73 us (3%)
    all_to_all x2, waiting for transfers between devices, exchange(): return lax.all_to_all(parts, axes, 0, 0)  44.6 us
    all_gather x1, blocking collectives, body(): all_v = lax.all_gather(own_v, DEPTH)  32 us
    all_to_all x2, starting transfers between devices, exchange(): return lax.all_to_all(parts, axes, 0, 0)  27.9 us
    all_to_all x2, blocking collectives, exchange(): return lax.all_to_all(parts, axes, 0, 0)  25.7 us
    all_gather x1, blocking collectives, body(): lax.all_gather(jnp.concatenate([own_z.reshape(32, 2 * k), own_g], axis=0)...  23.2 us
    dot_general x2, matrix products, contract_last(): lax.dot_general(left, right, (((1,), (1,)), ((), ())), precision=precisio...  7.19 us
    dot_general x9, matrix products, matmul(): jnp.dot(left, right, precision=precision, preferred_element_type=jnp.floa...  6.35 us
    slice x2, local copies, waits for them, and re-layouts, spread(): row_rows = got[:, 32:48].reshape(512, width)  3.93 us
  transfers between devices with their start and end apart: 2, of which 2 were waited for; matrix products, arithmetic and copies ran while one was open for 0% of the time, Pallas kernels for 0%

profile of v1, /device:TPU:1, one launch (start us, length us, event | category | flops | bytes accessed | tf_op | source)
XLA Modules:
  0.0 186.0 jit_solution(1944651175858359420)
XLA Ops:
  0.0 0.7 fusion.65
  0.7 5.9 %all_to_all.20 = f32[2,16,256]{2,1,0:T(8,128)S(1)} all-to-all(f32[2,16,256]{2,1,0:T(8,128)S(1)} %pad_maximum_fusion.4), channel_id=1, replica_groups=mesh['x_lo'=2,'z'=16,'y'=4,'x_hi'=2,'core'=2] {'x_lo'}, dimensions={0} | all-to-all | bytes 65536 | tf_op jit(solution)/shard_map/all_to_all | solution.py:29
  6.6 32.0 %all-gather = f32[32,16,256]{2,1,0:T(8,128)S(1)} all-gather(f32[2,16,256]{2,1,0:T(8,128)S(1)} %all_to_all.20), channel_id=2, replica_groups=mesh['x_lo'=2,'z'=16,'y'=4,'x_hi'=2,'core'=2] {'z'}, dimensions={0}, use_global_device_ids=true | all-gather | bytes 557056 | tf_op jit(solution)/shard_map/all_gather | solution.py:70
  38.7 0.1 broadcast_in_dim.16
  38.8 0.1 broadcast_in_dim.15
  38.9 1.3 pad_maximum_fusion.1
  40.2 15.5 %all-to-all-start.1 = ((f32[32,48,256]{2,1,0:T(8,128)}), f32[32,48,256]{2,1,0:T(8,128)}, u32[]{:S(2)}, u32[]{:S(2)}) async-start(f32[32,48,256]{2,1,0:T(8,128)} %bitcast.5), calls=%async_computation.1 | async-start | bytes 3145728 | tf_op jit(solution)/shard_map/all_to_all | solution.py:29
  55.7 0.0 copy-start
  55.7 0.2 fusion.43
  56.0 20.9 %all-to-all-done.1 = f32[32,48,256]{2,1,0:T(8,128)} async-done(((f32[32,48,256]{2,1,0:T(8,128)}), f32[32,48,256]{2,1,0:T(8,128)}, u32[]{:S(2)}, u32[]{:S(2)}) %all-to-all-start.1) | async-done | bytes 1572896 | tf_op jit(solution)/shard_map/all_to_all | solution.py:29
  76.9 1.5 fusion.63
  78.4 0.0 copy-start.1
  78.4 1.9 %fusion.12 = f32[256,512]{1,0:T(8,128)S(1)} fusion(f32[512,1024]{1,0:T(8,128)S(1)} %copy-done, f32[512,256]{1,0:T(8,128)S(1)} %bitcast.81, f32[512,256]{1,0:T(8,128)S(1)} %bitcast.83), kind=kOutput, calls=%fused_computation.22 | convolution fusion | flops 805568512 | bytes 3670016 | tf_op jit(solution)/shard_map/dot_general | solution.py:13
  80.3 0.0 copy-start.3
  80.3 0.6 fusion.66
  81.0 0.2 copy-done.3
  81.1 2.0 %copy.32 = f32[512,256]{1,0:T(8,128)} copy(f32[512,256]{0,1:T(8,128)} %bitcast.85) | data formatting | bytes 1048576 | tf_op jit(solution)/shard_map/dot_general | solution.py:13
  83.2 1.1 pad_maximum_fusion.2
  84.3 19.8 %all_to_all.21 = f32[32,24,256]{2,1,0:T(8,128)} all-to-all(f32[32,24,256]{2,1,0:T(8,128)S(1)} %pad_maximum_fusion.2), channel_id=1, replica_groups=mesh['x_lo'=2,'z'=16,'y'=4,'x_hi'=2,'core'=2] {'y','x_hi','core','x_lo'}, dimensions={0} | all-to-all | bytes 1572864 | tf_op jit(solution)/shard_map/all_to_all | solution.py:29
  104.1 1.2 reduce_sum.27
  105.3 23.2 %all-gather.1 = f32[640,256]{1,0:T(8,128)S(1)} all-gather(f32[40,256]{1,0:T(8,128)S(1)} %pad_maximum_fusion.3), channel_id=3, replica_groups=mesh['x_lo'=2,'z'=16,'y'=4,'x_hi'=2,'core'=2] {'z'}, dimensions={0}, use_global_device_ids=true | all-gather | bytes 696320 | tf_op jit(solution)/shard_map/all_gather | solution.py:83
  128.7 0.1 broadcast_in_dim.38
  128.7 0.1 broadcast_in_dim.18
  128.8 1.4 pad_maximum_fusion
  130.2 12.5 %all-to-all-start.3 = ((f32[32,56,256]{2,1,0:T(8,128)}), f32[32,56,256]{2,1,0:T(8,128)}, u32[]{:S(2)}, u32[]{:S(2)}) async-start(f32[32,56,256]{2,1,0:T(8,128)} %bitcast.80), calls=%async_computation.3 | async-start | bytes 3670016 | tf_op jit(solution)/shard_map/all_to_all | solution.py:29
  142.7 0.1 copy.45
  142.8 0.1 copy.44
  142.9 23.7 %all-to-all-done.3 = f32[32,56,256]{2,1,0:T(8,128)} async-done(((f32[32,56,256]{2,1,0:T(8,128)}), f32[32,56,256]{2,1,0:T(8,128)}, u32[]{:S(2)}, u32[]{:S(2)}) %all-to-all-start.3) | async-done | bytes 1835040 | tf_op jit(solution)/shard_map/all_to_all | solution.py:29
  166.6 1.0 slice_bitcast_fusion
  167.5 0.3 fusion.35
  167.8 0.3 convolution_negate_fusion.1
  168.1 0.3 convolution_subtract_fusion.1
  168.4 0.3 convolution_bitcast_fusion
  168.7 0.2 fusion.25
  168.9 1.2 fusion.20
  170.1 2.4 %fusion.62 = (f32[32,16,256]{2,1,0:T(8,128)S(1)}, f32[32,16,256]{2,1,0:T(8,128)}, f32[32,16,256]{2,1,0:T(8,128)}) fusion(f32[32,56,256]{2,1,0:T(8,128)} %all-to-all-done.3), kind=kLoop, calls=%fused_computation.83 | loop fusion | bytes 3145728 | tf_op jit(solution)/shard_map/slice | solution.py:42
  172.6 1.2 fusion.19
  173.8 0.3 convolution_multiply_fusion.1
  174.1 0.3 convolution_add_fusion.2
  174.4 0.3 convolution_add_fusion.1
  174.7 0.3 convolution_negate_fusion
  175.0 0.3 convolution_subtract_fusion
  175.3 0.2 fusion.28
  175.5 0.3 fusion.11
  175.8 0.7 select_maximum_fusion
  176.5 1.8 copy.39
  178.3 1.7 convolution_add_fusion
  180.0 6.0 %fusion.8 = f32[512,1024]{1,0:T(8,128)} fusion(f32[512,1024]{1,0:T(8,128)S(1)} %copy-done, f32[512,256]{1,0:T(8,128)S(1)} %bitcast.82, f32[512,256]{1,0:T(8,128)S(1)} %bitcast.84, f32[512,256]{1,0:T(8,128)S(1)} %bitcast.89, f32[512,256]{1,0:T(8,128)} %bitcast.90, f32[512,256]{0,1:T(8,128)S(1)} %convolution_add_fusion, f32[512,256]{0,1:T(8,128)S(1)} %copy-done.5), kind=kOutput, calls=%fused_computation.9 | convolution fusion | flops 1612972032 | bytes 7340032 | tf_op jit(solution)/shard_map/dot_general | solution.py:23
  (23 shorter events, 0.2 us)
Async XLA Ops:
  40.2 36.7 %all-to-all-start.1 = ((f32[32,48,256]{2,1,0:T(8,128)}), f32[32,48,256]{2,1,0:T(8,128)}, u32[]{:S(2)}, u32[]{:S(2)}) async-start(f32[32,48,256]{2,1,0:T(8,128)} %bitcast.5), calls=%async_computation.1 | async-start | bytes 3145728 | tf_op jit(solution)/shard_map/all_to_all | solution.py:29
  55.7 22.7 %copy-start = (f32[512,1024]{1,0:T(8,128)S(1)}, f32[512,1024]{1,0:T(8,128)}, u32[]{:S(2)}) copy-start(f32[512,1024]{1,0:T(8,128)} %param.3) | copy-start | bytes 6291460
  78.4 2.5 %copy-start.1 = (f32[32,16,256]{2,1,0:T(8,128)}, f32[32,16,256]{2,1,0:T(8,128)S(1)}, u32[]{:S(2)}) copy-start(f32[32,16,256]{2,1,0:T(8,128)S(1)} %get-tuple-element.10) | copy-start | bytes 1572868
  80.3 0.8 copy-start.3
  130.2 12.5 %copy-start.4 = (f32[2,128,128]{2,1,0:T(8,128)S(1)}, f32[2,128,128]{2,1,0:T(8,128)}, u32[]{:S(2)}) copy-start(f32[2,128,128]{2,1,0:T(8,128)} %param.5) | copy-start | bytes 393220
  130.2 36.4 %all-to-all-start.3 = ((f32[32,56,256]{2,1,0:T(8,128)}), f32[32,56,256]{2,1,0:T(8,128)}, u32[]{:S(2)}, u32[]{:S(2)}) async-start(f32[32,56,256]{2,1,0:T(8,128)} %bitcast.80), calls=%async_computation.3 | async-start | bytes 3670016 | tf_op jit(solution)/shard_map/all_to_all | solution.py:29
  178.3 1.7 copy-start.2
  178.3 1.7 copy-start.5
  178.3 1.7 copy-start.6

commit v2 on v1

v2 whole, which is shorter than its diff:
```python
import functools

import jax
import jax.numpy as jnp
from jax import lax
from jax.experimental import pallas as pl
from jax.experimental.pallas import tpu as pltpu
from jax.sharding import Mesh, PartitionSpec as P

DEPTH = "z"
PLANE = ("y", "x_hi", "core", "x_lo")
LIMIT = 48 * 1024 * 1024
CHUNKS = 4


def split(value):
    high = value.astype(jnp.bfloat16)
    return high, (value - high.astype(jnp.float32)).astype(jnp.bfloat16)


def product(left, right, dims):
    dot = functools.partial(
        lax.dot_general, dimension_numbers=(dims, ((), ())), preferred_element_type=jnp.float32
    )
    return dot(left[0], right[0]) + (dot(left[0], right[1]) + dot(left[1], right[0]))


def mm(left, right):
    return product(split(left), split(right), ((1,), (0,)))


def tm(left, right):
    return mm(left.T, right)


def mt(left, right):
    return product(split(left), split(right), ((1,), (1,)))


def part_kernel(matrix, got, own, message):
    k = own.shape[-1] // 2
    v0 = got[:, 0:16].reshape(512, 2 * k)
    v1 = got[:, 16:32].reshape(512, 2 * k)
    vr = got[:, 32:48].reshape(512, 2 * k)
    part = mm(matrix[:, :512], v0) + mm(matrix[:, 512:], v1)
    message[:, 0:16] = part.reshape(32, 16, 2 * k)
    gram = tm(vr, part)
    cross = tm(own[:, :k], own[:, k:])
    low = jnp.concatenate([cross, gram[k:, k:]], axis=1)
    message[0:16, 16:24] = gram[:k].reshape(16, 8, 2 * k)
    message[16:32, 16:24] = low.reshape(16, 8, 2 * k)


def update_kernel(matrix, got_v, got_z, factors, out, held, sems):
    k = factors.shape[-1]
    f1, f2 = factors[0], factors[1]
    gram = got_z[:, 48:56].reshape(2 * k, 2 * k)
    g11, g12, h12, g22 = gram[:k, :k], gram[:k, k:], gram[k:, :k], gram[k:, k:]
    b1 = -0.5 * tm(f1, mm(g11, f1))
    fh = mm(f1, h12)
    bh = mm(b1, h12)
    m = tm(f1, g12) + tm(b1, h12)
    c = m + bh
    s2 = mm(g22 - tm(g12, fh) - tm(h12, c), f2)
    b2 = -0.5 * tm(f2, s2)
    p12 = -mm(fh, f2)
    q12 = -mm(c, f2)
    zero = jnp.zeros_like(f1)
    p = split(jnp.concatenate([jnp.concatenate([f1, p12], axis=1), jnp.concatenate([zero, f2], axis=1)], axis=0))
    both = split(
        jnp.concatenate(
            [jnp.concatenate([b1 + b1.T, q12], axis=1), jnp.concatenate([q12.T, b2 + b2.T], axis=1)], axis=0
        )
    )
    v0 = split(got_v[:, 0:16].reshape(512, 2 * k))
    v1 = split(got_v[:, 16:32].reshape(512, 2 * k))
    z0 = split(got_z[:, 0:16].reshape(512, 2 * k))
    z1 = split(got_z[:, 16:32].reshape(512, 2 * k))
    last, inner = ((1,), (1,)), ((1,), (0,))
    rows = 512 // CHUNKS
    parts = 32 // CHUNKS
    copies = []
    for i in range(CHUNKS):
        here = slice(i * rows, (i + 1) * rows)
        vr = split(got_v[i * parts : (i + 1) * parts, 32:48].reshape(rows, 2 * k))
        zr = split(got_z[i * parts : (i + 1) * parts, 32:48].reshape(rows, 2 * k))
        on_z = split(product(vr, p, last))
        on_v = split(product(zr, p, inner) + product(vr, both, inner))
        held[here, :512] = matrix[here, :512] - product(on_z, z0, last) - product(on_v, v0, last)
        held[here, 512:] = matrix[here, 512:] - product(on_z, z1, last) - product(on_v, v1, last)
        copy = pltpu.make_async_copy(held.at[pl.ds(i * rows, rows)], out.at[pl.ds(i * rows, rows)], sems.at[i])
        copy.start()
        copies.append(copy)
    for copy in copies:
        copy.wait()


def part_of(matrix, got, own, interpret=False):
    return pl.pallas_call(
        part_kernel,
        out_shape=jax.ShapeDtypeStruct((32, 24, own.shape[-1]), jnp.float32),
        in_specs=[pl.BlockSpec(memory_space=pltpu.VMEM)] * 3,
        out_specs=pl.BlockSpec(memory_space=pltpu.VMEM),
        compiler_params=pltpu.CompilerParams(vmem_limit_bytes=LIMIT),
        interpret=interpret,
    )(matrix, got, own)


def updated_of(matrix, got_v, got_z, factors, interpret=False):
    return pl.pallas_call(
        update_kernel,
        out_shape=jax.ShapeDtypeStruct(matrix.shape, jnp.float32),
        in_specs=[pl.BlockSpec(memory_space=pltpu.VMEM)] * 4,
        out_specs=pl.BlockSpec(memory_space=pl.ANY),
        scratch_shapes=[pltpu.VMEM(matrix.shape, jnp.float32), pltpu.SemaphoreType.DMA((CHUNKS,))],
        compiler_params=pltpu.CompilerParams(vmem_limit_bytes=LIMIT),
        interpret=interpret,
    )(matrix, got_v, got_z, factors)


def exchange(parts, axes):
    return lax.all_to_all(parts, axes, 0, 0)


def spread(stack, own, extra=None):
    width = stack.shape[-1]
    cols = stack.reshape(8, 2, 2, 16, width).transpose(2, 0, 1, 3, 4).reshape(16, 1, 32, width)
    pieces = [jnp.broadcast_to(cols, (16, 2, 32, width)), jnp.broadcast_to(own[None], (16, 2, 16, width))]
    if extra is not None:
        pieces.append(jnp.broadcast_to(extra[None, None], (16, 2) + extra.shape))
    message = jnp.concatenate(pieces, axis=2)
    return exchange(message.reshape((32,) + message.shape[2:]), PLANE)


def body(matrix, vectors, factors):
    k = vectors.shape[-1]
    mine = jnp.concatenate([vectors[0], vectors[1]], axis=1)
    own_v = exchange(mine.reshape(2, 16, 2 * k), "x_lo")
    got_v = spread(lax.all_gather(own_v, DEPTH), own_v)
    sums = exchange(part_of(matrix, got_v, own_v.reshape(32, 2 * k)), PLANE)
    sums = jnp.sum(sums.reshape(16, 2, 24, 2 * k), axis=0)
    own_z = sums[:, :16]
    own_g = jnp.sum(sums[:, 16:], axis=0)
    gathered = lax.all_gather(jnp.concatenate([own_z.reshape(32, 2 * k), own_g], axis=0), DEPTH)
    got_z = spread(gathered[:, :32].reshape(16, 2, 16, 2 * k), own_z, jnp.sum(gathered[:, 32:], axis=0))
    return updated_of(matrix, got_v, got_z, factors)


def solution(mesh):
    fine = Mesh(mesh.devices.reshape(2, 16, 4, 2, 2), ("x_lo", "z", "y", "x_hi", "core"))
    row, col = ("x_lo", "z"), ("y", "x_hi", "core")
    in_specs = (P(row, col), P(None, row + col, None), P())
    return jax.shard_map(body, mesh=fine, in_specs=in_specs, out_specs=P(row, col), check_vma=False)
```

time: 188 us -> 164 us (0.87)
  blocking collectives: 80.9 us -> 153 us
  waiting for transfers between devices: 44.6 us -> 0 us
  starting transfers between devices: 27.9 us -> 0 us
  matrix products: 16.1 us -> 0 us
  local copies, waits for them, and re-layouts: 10.3 us -> 1.23 us
  Pallas kernels: 0 us -> 8.48 us
  other arithmetic: 5.73 us -> 0.36 us
    all_to_all x2 -> x4, blocking collectives: 25.7 us -> 98 us  [exchange(): return lax.all_to_all(parts, axes, 0, 0)]
    all_to_all x2 -> x0, waiting for transfers between devices: 44.6 us -> none  [exchange(): return lax.all_to_all(parts, axes, 0, 0)]
    all_to_all x2 -> x0, starting transfers between devices: 27.9 us -> none  [exchange(): return lax.all_to_all(parts, axes, 0, 0)]
    dot_general x19 -> x0, matrix products: 16.1 us -> none  [the longest x2 7.19 us: contract_last(): lax.dot_general(left, right, (((1,), (1,)), ((), ())), precision=precisio...]
    pallas_call x0 -> x2, Pallas kernels: none -> 8.48 us  [the longest x1 6.76 us: updated_of(): pl.pallas_call(update_kernel, out_shape=jax.ShapeDtypeStruct(matrix.shape...]
    slice x6 -> x1, local copies, waits for them, and re-layouts: 4 us -> 0.05 us  [body(): gathered[:, :32].reshape(16, 2, 16, 2 * k)]
    concatenate x2, other arithmetic: 2.67 us -> 0.27 us  [spread(): message = jnp.concatenate(pieces, axis=2)]
    dot_general x1 -> x0, local copies, waits for them, and re-layouts: 2.04 us -> none  [matmul(): jnp.dot(left, right, precision=precision, preferred_element_type=jnp.floa...]
  transfers between devices with their start and end apart: 2 -> 0, of which waited for: 2 -> 0; matrix products, arithmetic and copies ran while one was open for 0% -> 0% of each run, Pallas kernels for 0% -> 0%
where the time goes in v2:
time: 164 us; the launch traced here: 163 us
  blocking collectives  153 us (93%)
  Pallas kernels  8.48 us (5%)
    all_to_all x4, blocking collectives, exchange(): return lax.all_to_all(parts, axes, 0, 0)  98 us
    all_gather x1, blocking collectives, body(): got_v = spread(lax.all_gather(own_v, DEPTH), own_v)  32 us
    all_gather x1, blocking collectives, body(): lax.all_gather(jnp.concatenate([own_z.reshape(32, 2 * k), own_g], axis=0)...  23.2 us
    pallas_call x1, Pallas kernels, updated_of(): pl.pallas_call(update_kernel, out_shape=jax.ShapeDtypeStruct(matrix.shape...  6.76 us

profile of v2, /device:TPU:1, one launch (start us, length us, event | category | flops | bytes accessed | tf_op | source)
XLA Modules:
  0.0 163.5 jit_solution(15128337433690194384)
XLA Ops:
  0.0 0.7 fusion
  0.7 5.9 %all_to_all.20 = f32[2,16,256]{2,1,0:T(8,128)S(1)} all-to-all(f32[2,16,256]{2,1,0:T(8,128)S(1)} %pad_maximum_fusion.3), channel_id=1, replica_groups=mesh['x_lo'=2,'z'=16,'y'=4,'x_hi'=2,'core'=2] {'x_lo'}, dimensions={0} | all-to-all | bytes 65536 | tf_op jit(solution)/shard_map/all_to_all | solution.py:122
  6.6 32.0 %all-gather = f32[32,16,256]{2,1,0:T(8,128)S(1)} all-gather(f32[2,16,256]{2,1,0:T(8,128)S(1)} %all_to_all.20), channel_id=2, replica_groups=mesh['x_lo'=2,'z'=16,'y'=4,'x_hi'=2,'core'=2] {'z'}, dimensions={0}, use_global_device_ids=true | all-gather | bytes 557056 | tf_op jit(solution)/shard_map/all_gather | solution.py:139
  38.7 0.1 broadcast_in_dim.16
  38.8 0.1 broadcast_in_dim.15
  38.9 0.1 pad_maximum_fusion.1
  39.0 0.0 copy-start
  39.0 37.0 %all_to_all.21.got.got_v = f32[32,48,256]{2,1,0:T(8,128)S(1)} all-to-all(f32[32,48,256]{2,1,0:T(8,128)S(1)} %bitcast.18), channel_id=1, replica_groups=mesh['x_lo'=2,'z'=16,'y'=4,'x_hi'=2,'core'=2] {'y','x_hi','core','x_lo'}, dimensions={0} | all-to-all | bytes 3145728 | tf_op jit(solution)/shard_map/all_to_all | solution.py:122
  76.0 0.0 copy-done
  76.0 1.7 %shard_map.37 = f32[32,24,256]{2,1,0:T(8,128)S(1)} custom-call(f32[512,1024]{1,0:T(8,128)S(1)} %copy-done, f32[32,48,256]{2,1,0:T(8,128)S(1)} %all_to_all.21.got.got_v, f32[32,256]{1,0:T(8,128)S(1)} %bitcast.16), custom_call_target="tpu_custom_call" | custom-call | tf_op jit(solution)/shard_map/pallas_call | solution.py:99
  77.7 18.5 %all_to_all.22 = f32[32,24,256]{2,1,0:T(8,128)S(1)} all-to-all(f32[32,24,256]{2,1,0:T(8,128)S(1)} %shard_map.37), channel_id=1, replica_groups=mesh['x_lo'=2,'z'=16,'y'=4,'x_hi'=2,'core'=2] {'y','x_hi','core','x_lo'}, dimensions={0} | all-to-all | bytes 1572864 | tf_op jit(solution)/shard_map/all_to_all | solution.py:122
  96.2 0.1 reduce_sum.27
  96.3 23.2 %all-gather.1 = f32[640,256]{1,0:T(8,128)S(1)} all-gather(f32[40,256]{1,0:T(8,128)S(1)} %pad_maximum_fusion.2), channel_id=3, replica_groups=mesh['x_lo'=2,'z'=16,'y'=4,'x_hi'=2,'core'=2] {'z'}, dimensions={0}, use_global_device_ids=true | all-gather | bytes 696320 | tf_op jit(solution)/shard_map/all_gather | solution.py:144
  119.6 0.1 broadcast_in_dim.37
  119.7 0.1 broadcast_in_dim.36
  119.8 0.2 pad_maximum_fusion
  120.0 0.0 copy-start.1
  120.0 0.0 copy-start.2
  120.0 36.7 %all_to_all.23.got_z = f32[32,56,256]{2,1,0:T(8,128)S(1)} all-to-all(f32[32,56,256]{2,1,0:T(8,128)S(1)} %bitcast.17), channel_id=1, replica_groups=mesh['x_lo'=2,'z'=16,'y'=4,'x_hi'=2,'core'=2] {'y','x_hi','core','x_lo'}, dimensions={0} | all-to-all | bytes 3670016 | tf_op jit(solution)/shard_map/all_to_all | solution.py:122
  156.7 0.0 copy-done.1
  156.7 0.0 copy-done.2
  156.7 6.8 %shard_map.38 = f32[512,1024]{1,0:T(8,128)} custom-call(f32[512,1024]{1,0:T(8,128)S(1)} %copy-done.1, f32[32,48,256]{2,1,0:T(8,128)S(1)} %all_to_all.21.got.got_v, f32[32,56,256]{2,1,0:T(8,128)S(1)} %all_to_all.23.got_z, f32[2,128,128]{2,1,0:T(8,128)S(1)} %copy-done.2), custom_call_target="tpu_custom_call" | custom-call | tf_op jit(solution)/shard_map/pallas_call | solution.py:110
  (9 shorter events, 0.2 us)
Async XLA Ops:
  39.0 37.0 %copy-start = (f32[512,1024]{1,0:T(8,128)S(1)}, f32[512,1024]{1,0:T(8,128)}, u32[]{:S(2)}) copy-start(f32[512,1024]{1,0:T(8,128)} %matrix.3) | copy-start | bytes 6291460
  120.0 36.7 %copy-start.1 = (f32[512,1024]{1,0:T(8,128)S(1)}, f32[512,1024]{1,0:T(8,128)}, u32[]{:S(2)}) copy-start(f32[512,1024]{1,0:T(8,128)} %matrix.3) | copy-start | bytes 6291460
  120.0 36.7 %copy-start.2 = (f32[2,128,128]{2,1,0:T(8,128)S(1)}, f32[2,128,128]{2,1,0:T(8,128)}, u32[]{:S(2)}) copy-start(f32[2,128,128]{2,1,0:T(8,128)} %factors.1) | copy-start | bytes 393220

commit v3 on v0

v3 whole, which is shorter than its diff:
```python
import jax
import jax.numpy as jnp
from jax import lax
from jax.experimental import pallas as pl
from jax.experimental.pallas import tpu as pltpu
from jax.sharding import Mesh, PartitionSpec as P

COL = ("y", "x_hi", "core")
PLANE = COL + ("x_lo",)
RINGS = [[2 * z + (z + first) % 2 for z in range(16)] for first in range(2)]
LIMIT = 48 * 1024 * 1024
CHUNKS = 4
LAST, INNER = 1, 0


def split(value):
    high = value.astype(jnp.bfloat16)
    return high, (value - high.astype(jnp.float32)).astype(jnp.bfloat16)


def product(left, right, along):
    left, right = [split(a) for a in left], [split(b) for b in right]
    wide = [a[0] for a in left] + [a[1] for a in left] + [a[0] for a in left]
    tall = [b[0] for b in right] + [b[0] for b in right] + [b[1] for b in right]
    return lax.dot_general(
        jnp.concatenate(wide, axis=1),
        jnp.concatenate(tall, axis=along),
        (((1,), (along,)), ((), ())),
        preferred_element_type=jnp.float32,
    )


def mm(left, right):
    return product([left], [right], INNER)


def in_order(got, first, size, swap):
    parts = []
    for chip in range(8):
        for core in range(2):
            at = 4 * chip + 2 * (swap if core == 0 else 1 - swap)
            parts.append(got[pl.ds(at, 2), first : first + size].reshape(2 * size, got.shape[-1]))
    return jnp.concatenate(parts, axis=0)


def part_kernel(odd, matrix, got, own, message):
    k = own.shape[-1] // 2
    v0 = in_order(got, 0, 16, odd[0])
    v1 = in_order(got, 16, 16, 1 - odd[0])
    part = product([matrix[:, :512], matrix[:, 512:]], [v0, v1], INNER)
    message[:, 0:16] = part.reshape(32, 16, 2 * k)
    row = got[:, 32:48].reshape(512, 2 * k)
    gram = mm(row.T, part)
    cross = mm(own[:, :k].T, own[:, k:])
    low = jnp.concatenate([cross, gram[k:, k:]], axis=1)
    pieces = jnp.concatenate([gram[:k], low], axis=0).reshape(16, 2, 8, 2 * k)
    for chip in range(8):
        message[pl.ds(4 * chip + 2 * odd[0], 2), 16:24] = pieces[2 * chip]
        message[pl.ds(4 * chip + 2 * (1 - odd[0]), 2), 16:24] = pieces[2 * chip + 1]


def update_kernel(odd, matrix, got_v, got_z, factors, out, held, sems):
    k = factors.shape[-1]
    f1, f2 = factors[0], factors[1]
    gram = in_order(got_z, 48, 8, odd[0])
    g11, g12, h12, g22 = gram[:k, :k], gram[:k, k:], gram[k:, :k], gram[k:, k:]
    p12 = -mm(mm(f1, h12), f2)
    p = jnp.concatenate(
        [jnp.concatenate([f1, p12], axis=1), jnp.concatenate([jnp.zeros_like(f1), f2], axis=1)], axis=0
    )
    full = jnp.concatenate([gram[:k], jnp.concatenate([g12.T, g22], axis=1)], axis=0)
    gp = mm(full, p)
    v0 = in_order(got_v, 0, 16, odd[0])
    v1 = in_order(got_v, 16, 16, 1 - odd[0])
    z0 = in_order(got_z, 0, 16, odd[0])
    z1 = in_order(got_z, 16, 16, 1 - odd[0])
    rows = 512 // CHUNKS
    parts = 32 // CHUNKS
    copies = []
    for i in range(CHUNKS):
        here = slice(i * rows, (i + 1) * rows)
        vr = got_v[i * parts : (i + 1) * parts, 32:48].reshape(rows, 2 * k)
        zr = got_z[i * parts : (i + 1) * parts, 32:48].reshape(rows, 2 * k)
        on_z = product([vr], [p], LAST)
        on_v = product([zr, on_z], [p, -gp], INNER)
        held[here, :512] = matrix[here, :512] - product([on_z, on_v], [z0, v0], LAST)
        held[here, 512:] = matrix[here, 512:] - product([on_z, on_v], [z1, v1], LAST)
        copy = pltpu.make_async_copy(held.at[pl.ds(i * rows, rows)], out.at[pl.ds(i * rows, rows)], sems.at[i])
        copy.start()
        copies.append(copy)
    for copy in copies:
        copy.wait()


def part_of(*args):
    return pl.pallas_call(
        part_kernel,
        out_shape=jax.ShapeDtypeStruct((32, 24, args[-1].shape[-1]), jnp.float32),
        in_specs=[pl.BlockSpec(memory_space=pltpu.SMEM)] + [pl.BlockSpec(memory_space=pltpu.VMEM)] * 3,
        out_specs=pl.BlockSpec(memory_space=pltpu.VMEM),
        compiler_params=pltpu.CompilerParams(vmem_limit_bytes=LIMIT),
    )(*args)


def updated_of(*args):
    shape = args[1].shape
    return pl.pallas_call(
        update_kernel,
        out_shape=jax.ShapeDtypeStruct(shape, jnp.float32),
        in_specs=[pl.BlockSpec(memory_space=pltpu.SMEM)] + [pl.BlockSpec(memory_space=pltpu.VMEM)] * 4,
        out_specs=pl.BlockSpec(memory_space=pl.ANY),
        scratch_shapes=[pltpu.VMEM(shape, jnp.float32), pltpu.SemaphoreType.DMA((CHUNKS,))],
        compiler_params=pltpu.CompilerParams(vmem_limit_bytes=LIMIT),
    )(*args)


def exchange(parts, axes):
    return lax.all_to_all(parts, axes, 0, 0)


def gather(piece):
    return lax.all_gather(piece, ("z", "core"), axis_index_groups=RINGS)


def spread(stack, *common):
    width = stack.shape[-1]
    cols = stack.reshape(8, 2, 2, 16, width).transpose(2, 0, 1, 3, 4).reshape(16, 1, 32, width)
    pieces = [jnp.broadcast_to(cols, (16, 2, 32, width))]
    pieces += [jnp.broadcast_to(c[None], (16, 2) + c.shape[1:]) for c in common]
    message = jnp.concatenate(pieces, axis=2)
    return exchange(message.reshape((32,) + message.shape[2:]), PLANE)


def body(matrix, vectors, factors):
    k = vectors.shape[-1]
    mine = jnp.concatenate([vectors[0], vectors[1]], axis=1)
    odd = (lax.axis_index("z") % 2).reshape(1)
    half = lax.axis_index("x_lo")
    halves = mine.reshape(2, 16, 2 * k)
    theirs = lax.ppermute(jnp.where(half == 0, halves[1], halves[0]), "x_lo", [(0, 1), (1, 0)])
    own_v = jnp.stack([jnp.where(half == 0, halves[0], theirs), jnp.where(half == 0, theirs, halves[1])])
    got_v = spread(gather(own_v), own_v)
    sums = exchange(part_of(odd, matrix, got_v, own_v.reshape(32, 2 * k)), PLANE)
    sums = jnp.sum(sums.reshape(16, 2, 24, 2 * k), axis=0)
    own_z = sums[:, :16]
    own_g = jnp.sum(sums[:, 16:], axis=0)
    gathered = gather(jnp.concatenate([own_z.reshape(32, 2 * k), own_g], axis=0))
    got_z = spread(gathered[:, :32].reshape(16, 2, 16, 2 * k), own_z, jnp.sum(gathered[:, 32:], axis=0)[None])
    return updated_of(odd, matrix, got_v, got_z, factors)


def solution(mesh):
    fine = Mesh(mesh.devices.reshape(2, 16, 4, 2, 2), ("x_lo", "z", "y", "x_hi", "core"))
    row = ("x_lo", "z")
    in_specs = (P(row, COL), P(None, row + COL, None), P())
    return jax.shard_map(body, mesh=fine, in_specs=in_specs, out_specs=P(row, COL), check_vma=False)
```

time: 1620 us -> 159 us (0.10); the launches traced: 1600 us -> 159 us
  waiting for transfers between devices: 1520 us -> 22.2 us
  blocking collectives: 29 us -> 113 us
  matrix products: 29.3 us -> 0 us
    psum x7 -> x0, waiting for transfers between devices: 1520 us -> none  [the longest x3 746 us: broadcast(): return lax.psum(kept, axis)]
    all_to_all x0 -> x2, blocking collectives: none -> 48.9 us  [exchange(): return lax.all_to_all(parts, axes, 0, 0)]
    all_gather x1 -> x2, blocking collectives: 29 us -> 63.7 us  [gather(): return lax.all_gather(piece, ('z', 'core'), axis_index_groups=RINGS)]
    dot_general x14 -> x0, matrix products: 29.3 us -> none  [the longest x4 12.4 us: contract_last(): lax.dot_general(left, right, (((1,), (1,)), ((), ())), precision=HIGH, pr...]
    all_to_all x0 -> x1, waiting for transfers between devices: none -> 21.1 us  [exchange(): return lax.all_to_all(parts, axes, 0, 0)]
  transfers between devices with their start and end apart: 7 -> 2, of which waited for: 7 -> 2; matrix products, arithmetic and copies ran while one was open for 0% -> 0% of each run, Pallas kernels for 0% -> 0%
where the time goes in v3:
time: 159 us
  blocking collectives  113 us (71%)
  waiting for transfers between devices  22.2 us (14%)
  starting transfers between devices  11.1 us (7%)
  Pallas kernels  8.21 us (5%)
  local copies, waits for them, and re-layouts  2.82 us (2%)
    all_gather x2, blocking collectives, gather(): return lax.all_gather(piece, ('z', 'core'), axis_index_groups=RINGS)  63.7 us
    all_to_all x2, blocking collectives, exchange(): return lax.all_to_all(parts, axes, 0, 0)  48.9 us
    all_to_all x1, waiting for transfers between devices, exchange(): return lax.all_to_all(parts, axes, 0, 0)  21.1 us
    all_to_all x1, starting transfers between devices, exchange(): return lax.all_to_all(parts, axes, 0, 0)  7.2 us
    pallas_call x1, Pallas kernels, updated_of(): pl.pallas_call(update_kernel, out_shape=jax.ShapeDtypeStruct(shape, jnp.f...  6.5 us
    ppermute x1, starting transfers between devices, body(): lax.ppermute(jnp.where(half == 0, halves[1], halves[0]), 'x_lo', [(0, 1),...  3.94 us
  transfers between devices with their start and end apart: 2, of which 2 were waited for; matrix products, arithmetic and copies ran while one was open for 0% of the time, Pallas kernels for 0%

profile of v3, /device:TPU:1, one launch (start us, length us, event | category | flops | bytes accessed | tf_op | source)
XLA Modules:
  0.0 158.6 jit_solution(14865094931985367883)
XLA Ops:
  0.0 0.7 slice_bitcast_fusion.1
  0.7 3.9 %collective-permute-start = (f32[16,256]{1,0:T(8,128)S(1)}, f32[16,256]{1,0:T(8,128)S(1)}, u32[]{:S(2)}, u32[]{:S(2)}) collective-permute-start(f32[16,256]{1,0:T(8,128)S(1)} %broadcast_select_fusion), channel_id=1, source_target_pairs={{0,256},{256,0},{1,257},{257,1},{2,258},{258,2},{3,259},{259,3},{4... | collective-permute-start | bytes 49160 | tf_op jit(solution)/shard_map/ppermute | solution.py:140
  4.7 1.1 collective-permute-done
  5.8 36.4 %all-gather = f32[32,16,256]{2,1,0:T(8,128)S(1)} all-gather(f32[2,16,256]{2,1,0:T(8,128)S(1)} %pad_maximum_fusion.3), channel_id=2, replica_groups={{0,17,32,49,64,81,96,113,128,145,160,177,192,209,224,241},{1,16,33,48,6..., dimensions={0}, use_global_device_ids=true | all-gather | bytes 557056 | tf_op jit(solution)/shard_map/all_gather | solution.py:122
  42.2 0.1 broadcast_in_dim.16
  42.3 0.1 broadcast_in_dim.15
  42.4 1.2 pad_maximum_fusion.1
  43.7 7.2 %all-to-all-start = ((f32[32,48,256]{2,1,0:T(8,128)}), f32[32,48,256]{2,1,0:T(8,128)S(1)}, u32[]{:S(2)}, u32[]{:S(2)}) async-start(f32[32,48,256]{2,1,0:T(8,128)} %bitcast.8), calls=%async_computation | async-start | bytes 3145728 | tf_op jit(solution)/shard_map/all_to_all | solution.py:118
  50.9 21.1 %all-to-all-done.got.got_v = f32[32,48,256]{2,1,0:T(8,128)S(1)} async-done(((f32[32,48,256]{2,1,0:T(8,128)}), f32[32,48,256]{2,1,0:T(8,128)S(1)}, u32[]{:S(2)}, u32[]{:S(2)}) %all-to-all-start) | async-done | bytes 1572896 | tf_op jit(solution)/shard_map/all_to_all | solution.py:118
  72.0 0.0 copy-start
  72.0 1.6 %copy-done = f32[512,1024]{1,0:T(8,128)S(1)} copy-done((f32[512,1024]{1,0:T(8,128)S(1)}, f32[512,1024]{1,0:T(8,128)}, u32[]{:S(2)}) %copy-start) | copy-done | bytes 2097176
  73.6 1.7 %shard_map.37 = f32[32,24,256]{2,1,0:T(8,128)S(1)} custom-call(s32[1]{0:T(128)} %bitcast.odd, f32[512,1024]{1,0:T(8,128)S(1)} %copy-done, f32[32,48,256]{2,1,0:T(8,128)S(1)} %all-to-all-done.got.got_v, f32[32,256]{1,0:T(8,128)S(1)} %bitcast.23), custom_call_target="tpu_custom_call" | custom-call | tf_op jit(solution)/shard_map/pallas_call | solution.py:96
  75.3 19.7 %all_to_all.15 = f32[32,24,256]{2,1,0:T(8,128)S(1)} all-to-all(f32[32,24,256]{2,1,0:T(8,128)S(1)} %shard_map.37), channel_id=1, replica_groups=mesh['x_lo'=2,'z'=16,'y'=4,'x_hi'=2,'core'=2] {'y','x_hi','core','x_lo'}, dimensions={0} | all-to-all | bytes 1572864 | tf_op jit(solution)/shard_map/all_to_all | solution.py:118
  95.0 0.1 reduce_sum.27
  95.1 27.3 %all-gather.1 = f32[640,256]{1,0:T(8,128)S(1)} all-gather(f32[40,256]{1,0:T(8,128)S(1)} %pad_maximum_fusion.2), channel_id=3, replica_groups={{0,17,32,49,64,81,96,113,128,145,160,177,192,209,224,241},{1,16,33,48,6..., dimensions={0}, use_global_device_ids=true | all-gather | bytes 696320 | tf_op jit(solution)/shard_map/all_gather | solution.py:122
  122.5 0.1 broadcast_in_dim.36
  122.6 0.1 broadcast_in_dim.35
  122.7 0.2 pad_maximum_fusion
  122.9 0.0 copy-start.1
  122.9 0.0 copy-start.2
  122.9 29.2 %all_to_all.16.got_z = f32[32,56,256]{2,1,0:T(8,128)S(1)} all-to-all(f32[32,56,256]{2,1,0:T(8,128)S(1)} %bitcast.24), channel_id=1, replica_groups=mesh['x_lo'=2,'z'=16,'y'=4,'x_hi'=2,'core'=2] {'y','x_hi','core','x_lo'}, dimensions={0} | all-to-all | bytes 3670016 | tf_op jit(solution)/shard_map/all_to_all | solution.py:118
  152.1 0.0 copy-done.1
  152.1 0.0 copy-done.2
  152.1 6.5 %shard_map.38 = f32[512,1024]{1,0:T(8,128)} custom-call(s32[1]{0:T(128)} %bitcast.odd, f32[512,1024]{1,0:T(8,128)S(1)} %copy-done.1, f32[32,48,256]{2,1,0:T(8,128)S(1)} %all-to-all-done.got.got_v, f32[32,56,256]{2,1,0:T(8,128)S(1)} %all_to_all.16.got_z, f32[2,128,128]{2,1,0:T(8,128)S(1)} %copy-done.2), custom_call_target="tpu_custom_call" | custom-call | tf_op jit(solution)/shard_map/pallas_call | solution.py:107
  (11 shorter events, 0.2 us)
Async XLA Ops:
  0.7 5.1 %collective-permute-start = (f32[16,256]{1,0:T(8,128)S(1)}, f32[16,256]{1,0:T(8,128)S(1)}, u32[]{:S(2)}, u32[]{:S(2)}) collective-permute-start(f32[16,256]{1,0:T(8,128)S(1)} %broadcast_select_fusion), channel_id=1, source_target_pairs={{0,256},{256,0},{1,257},{257,1},{2,258},{258,2},{3,259},{259,3},{4... | collective-permute-start | bytes 49160 | tf_op jit(solution)/shard_map/ppermute | solution.py:140
  43.7 28.3 %all-to-all-start = ((f32[32,48,256]{2,1,0:T(8,128)}), f32[32,48,256]{2,1,0:T(8,128)S(1)}, u32[]{:S(2)}, u32[]{:S(2)}) async-start(f32[32,48,256]{2,1,0:T(8,128)} %bitcast.8), calls=%async_computation | async-start | bytes 3145728 | tf_op jit(solution)/shard_map/all_to_all | solution.py:118
  72.0 1.6 %copy-start = (f32[512,1024]{1,0:T(8,128)S(1)}, f32[512,1024]{1,0:T(8,128)}, u32[]{:S(2)}) copy-start(f32[512,1024]{1,0:T(8,128)} %matrix.3) | copy-start | bytes 6291460
  122.9 29.2 %copy-start.1 = (f32[512,1024]{1,0:T(8,128)S(1)}, f32[512,1024]{1,0:T(8,128)}, u32[]{:S(2)}) copy-start(f32[512,1024]{1,0:T(8,128)} %matrix.3) | copy-start | bytes 6291460
  122.9 29.2 %copy-start.2 = (f32[2,128,128]{2,1,0:T(8,128)S(1)}, f32[2,128,128]{2,1,0:T(8,128)}, u32[]{:S(2)}) copy-start(f32[2,128,128]{2,1,0:T(8,128)} %factors.1) | copy-start | bytes 393220

commit v4 on v3

--- a/solution.py
+++ b/solution.py
@@ -19,11 +19,19 @@
 
 
 def product(left, right, along):
-    left, right = [split(a) for a in left], [split(b) for b in right]
-    wide = [a[0] for a in left] + [a[1] for a in left] + [a[0] for a in left]
+    return contract(thrice(left), right, along)
+
+
+def thrice(left):
+    left = [split(a) for a in left]
+    return jnp.concatenate([a[0] for a in left] + [a[1] for a in left] + [a[0] for a in left], axis=1)
+
+
+def contract(wide, right, along):
+    right = [split(b) for b in right]
     tall = [b[0] for b in right] + [b[0] for b in right] + [b[1] for b in right]
     return lax.dot_general(
-        jnp.concatenate(wide, axis=1),
+        wide,
         jnp.concatenate(tall, axis=along),
         (((1,), (along,)), ((), ())),
         preferred_element_type=jnp.float32,
@@ -34,9 +42,9 @@
     return product([left], [right], INNER)
 
 
-def in_order(got, first, size, swap):
+def in_order(got, first, size, swap, chip_from=0, chips=8):
     parts = []
-    for chip in range(8):
+    for chip in range(chip_from, chip_from + chips):
         for core in range(2):
             at = 4 * chip + 2 * (swap if core == 0 else 1 - swap)
             parts.append(got[pl.ds(at, 2), first : first + size].reshape(2 * size, got.shape[-1]))
@@ -70,22 +78,22 @@
     )
     full = jnp.concatenate([gram[:k], jnp.concatenate([g12.T, g22], axis=1)], axis=0)
     gp = mm(full, p)
-    v0 = in_order(got_v, 0, 16, odd[0])
-    v1 = in_order(got_v, 16, 16, 1 - odd[0])
-    z0 = in_order(got_z, 0, 16, odd[0])
-    z1 = in_order(got_z, 16, 16, 1 - odd[0])
-    rows = 512 // CHUNKS
-    parts = 32 // CHUNKS
+    on_z = product([got_v[:, 32:48].reshape(512, 2 * k)], [p], LAST)
+    on_v = product([got_z[:, 32:48].reshape(512, 2 * k), on_z], [p, -gp], INNER)
+    left = thrice([on_z, on_v])
+    chips = 16 // CHUNKS
+    wide = 64 * chips
     copies = []
     for i in range(CHUNKS):
-        here = slice(i * rows, (i + 1) * rows)
-        vr = got_v[i * parts : (i + 1) * parts, 32:48].reshape(rows, 2 * k)
-        zr = got_z[i * parts : (i + 1) * parts, 32:48].reshape(rows, 2 * k)
-        on_z = product([vr], [p], LAST)
-        on_v = product([zr, on_z], [p, -gp], INNER)
-        held[here, :512] = matrix[here, :512] - product([on_z, on_v], [z0, v0], LAST)
-        held[here, 512:] = matrix[here, 512:] - product([on_z, on_v], [z1, v1], LAST)
-        copy = pltpu.make_async_copy(held.at[pl.ds(i * rows, rows)], out.at[pl.ds(i * rows, rows)], sems.at[i])
+        half = 2 * i // CHUNKS
+        swap = odd[0] if half == 0 else 1 - odd[0]
+        first = i * chips - 8 * half
+        z_col = in_order(got_z, 16 * half, 16, swap, first, chips)
+        v_col = in_order(got_v, 16 * half, 16, swap, first, chips)
+        here = slice(i * wide, (i + 1) * wide)
+        held[:, here] = matrix[:, here] - contract(left, [z_col, v_col], LAST)
+        there = pl.ds(i * wide, wide)
+        copy = pltpu.make_async_copy(held.at[:, there], out.at[:, there], sems.at[i])
         copy.start()
         copies.append(copy)
     for copy in copies:
@@ -134,11 +142,12 @@
 def body(matrix, vectors, factors):
     k = vectors.shape[-1]
     mine = jnp.concatenate([vectors[0], vectors[1]], axis=1)
-    odd = (lax.axis_index("z") % 2).reshape(1)
+    odd = (lax.axis_index("z") & 1).reshape(1)
     half = lax.axis_index("x_lo")
     halves = mine.reshape(2, 16, 2 * k)
     theirs = lax.ppermute(jnp.where(half == 0, halves[1], halves[0]), "x_lo", [(0, 1), (1, 0)])
     own_v = jnp.stack([jnp.where(half == 0, halves[0], theirs), jnp.where(half == 0, theirs, halves[1])])
+    odd, own_v = lax.optimization_barrier((odd, own_v))
     got_v = spread(gather(own_v), own_v)
     sums = exchange(part_of(odd, matrix, got_v, own_v.reshape(32, 2 * k)), PLANE)
     sums = jnp.sum(sums.reshape(16, 2, 24, 2 * k), axis=0)

time: 159 us -> 153 us (0.962)
  blocking collectives: 113 us -> 140 us
  waiting for transfers between devices: 22.2 us -> 1.11 us
  starting transfers between devices: 11.1 us -> 3.94 us
  Pallas kernels: 8.21 us -> 5.51 us
    all_to_all x2 -> x3, blocking collectives: 48.9 us -> 76.4 us  [exchange(): return lax.all_to_all(parts, axes, 0, 0)]
    all_to_all x1 -> x0, waiting for transfers between devices: 21.1 us -> none  [exchange(): return lax.all_to_all(parts, axes, 0, 0)]
    all_to_all x1 -> x0, starting transfers between devices: 7.2 us -> none  [exchange(): return lax.all_to_all(parts, axes, 0, 0)]
    pallas_call x1, Pallas kernels: 6.5 us -> 3.81 us  [updated_of(): pl.pallas_call(update_kernel, out_shape=jax.ShapeDtypeStruct(shape, jnp.f...]
  transfers between devices with their start and end apart: 2 -> 1, of which waited for: 2 -> 1; matrix products, arithmetic and copies ran while one was open for 0% -> 0% of each run, Pallas kernels for 0% -> 0%
where the time goes in v4:
time: 153 us; the launch traced here: 152 us
  blocking collectives  140 us (92%)
  Pallas kernels  5.51 us (4%)
  starting transfers between devices  3.94 us (3%)
    all_to_all x3, blocking collectives, exchange(): return lax.all_to_all(parts, axes, 0, 0)  76.4 us
    all_gather x2, blocking collectives, gather(): return lax.all_gather(piece, ('z', 'core'), axis_index_groups=RINGS)  63.6 us
    ppermute x1, starting transfers between devices, body(): lax.ppermute(jnp.where(half == 0, halves[1], halves[0]), 'x_lo', [(0, 1),...  3.94 us
    pallas_call x1, Pallas kernels, updated_of(): pl.pallas_call(update_kernel, out_shape=jax.ShapeDtypeStruct(shape, jnp.f...  3.81 us
  transfers between devices with their start and end apart: 1, of which 1 were waited for; matrix products, arithmetic and copies ran while one was open for 0% of the time, Pallas kernels for 0%

profile of v4, /device:TPU:1, one launch (start us, length us, event | category | flops | bytes accessed | tf_op | source)
XLA Modules:
  0.0 152.4 jit_solution(15313135784299182873)
XLA Ops:
  0.0 0.7 slice_bitcast_fusion.1
  0.7 3.9 %collective-permute-start = (f32[16,256]{1,0:T(8,128)S(1)}, f32[16,256]{1,0:T(8,128)S(1)}, u32[]{:S(2)}, u32[]{:S(2)}) collective-permute-start(f32[16,256]{1,0:T(8,128)S(1)} %broadcast_select_fusion), channel_id=1, source_target_pairs={{0,256},{256,0},{1,257},{257,1},{2,258},{258,2},{3,259},{259,3},{4... | collective-permute-start | bytes 49160 | tf_op jit(solution)/shard_map/ppermute | solution.py:148
  4.7 1.1 collective-permute-done
  5.8 36.4 %all-gather = f32[32,16,256]{2,1,0:T(8,128)S(1)} all-gather(f32[2,16,256]{2,1,0:T(8,128)S(1)} %pad_maximum_fusion.3), channel_id=2, replica_groups={{0,17,32,49,64,81,96,113,128,145,160,177,192,209,224,241},{1,16,33,48,6..., dimensions={0}, use_global_device_ids=true | all-gather | bytes 557056 | tf_op jit(solution)/shard_map/all_gather | solution.py:130
  42.2 0.1 broadcast_in_dim.16
  42.3 0.1 broadcast_in_dim.15
  42.4 0.2 pad_maximum_fusion.1
  42.6 0.0 copy-start
  42.6 28.8 %all_to_all.15.got.got_v = f32[32,48,256]{2,1,0:T(8,128)S(1)} all-to-all(f32[32,48,256]{2,1,0:T(8,128)S(1)} %bitcast.25), channel_id=1, replica_groups=mesh['x_lo'=2,'z'=16,'y'=4,'x_hi'=2,'core'=2] {'y','x_hi','core','x_lo'}, dimensions={0} | all-to-all | bytes 3145728 | tf_op jit(solution)/shard_map/all_to_all | solution.py:126
  71.4 0.0 copy-done
  71.4 1.7 %shard_map.37 = f32[32,24,256]{2,1,0:T(8,128)S(1)} custom-call(s32[1]{0:T(128)} %bitcast.odd, f32[512,1024]{1,0:T(8,128)S(1)} %copy-done, f32[32,48,256]{2,1,0:T(8,128)S(1)} %all_to_all.15.got.got_v, f32[32,256]{1,0:T(8,128)S(1)} %bitcast.23), custom_call_target="tpu_custom_call" | custom-call | tf_op jit(solution)/shard_map/pallas_call | solution.py:104
  73.1 18.5 %all_to_all.16 = f32[32,24,256]{2,1,0:T(8,128)S(1)} all-to-all(f32[32,24,256]{2,1,0:T(8,128)S(1)} %shard_map.37), channel_id=1, replica_groups=mesh['x_lo'=2,'z'=16,'y'=4,'x_hi'=2,'core'=2] {'y','x_hi','core','x_lo'}, dimensions={0} | all-to-all | bytes 1572864 | tf_op jit(solution)/shard_map/all_to_all | solution.py:126
  91.5 0.1 reduce_sum.27
  91.6 27.2 %all-gather.1 = f32[640,256]{1,0:T(8,128)S(1)} all-gather(f32[40,256]{1,0:T(8,128)S(1)} %pad_maximum_fusion.2), channel_id=3, replica_groups={{0,17,32,49,64,81,96,113,128,145,160,177,192,209,224,241},{1,16,33,48,6..., dimensions={0}, use_global_device_ids=true | all-gather | bytes 696320 | tf_op jit(solution)/shard_map/all_gather | solution.py:130
  119.0 0.1 broadcast_in_dim.36
  119.1 0.1 broadcast_in_dim.35
  119.2 0.2 pad_maximum_fusion
  119.4 0.0 copy-start.1
  119.4 0.0 copy-start.2
  119.4 29.2 %all_to_all.17.got_z = f32[32,56,256]{2,1,0:T(8,128)S(1)} all-to-all(f32[32,56,256]{2,1,0:T(8,128)S(1)} %bitcast.24), channel_id=1, replica_groups=mesh['x_lo'=2,'z'=16,'y'=4,'x_hi'=2,'core'=2] {'y','x_hi','core','x_lo'}, dimensions={0} | all-to-all | bytes 3670016 | tf_op jit(solution)/shard_map/all_to_all | solution.py:126
  148.6 0.0 copy-done.1
  148.6 0.0 copy-done.2
  148.6 3.8 %shard_map.38 = f32[512,1024]{1,0:T(8,128)} custom-call(s32[1]{0:T(128)} %bitcast.odd, f32[512,1024]{1,0:T(8,128)S(1)} %copy-done.1, f32[32,48,256]{2,1,0:T(8,128)S(1)} %all_to_all.15.got.got_v, f32[32,56,256]{2,1,0:T(8,128)S(1)} %all_to_all.17.got_z, f32[2,128,128]{2,1,0:T(8,128)S(1)} %copy-done.2), custom_call_target="tpu_custom_call" | custom-call | tf_op jit(solution)/shard_map/pallas_call | solution.py:115
  (11 shorter events, 0.2 us)
Async XLA Ops:
  0.7 5.1 %collective-permute-start = (f32[16,256]{1,0:T(8,128)S(1)}, f32[16,256]{1,0:T(8,128)S(1)}, u32[]{:S(2)}, u32[]{:S(2)}) collective-permute-start(f32[16,256]{1,0:T(8,128)S(1)} %broadcast_select_fusion), channel_id=1, source_target_pairs={{0,256},{256,0},{1,257},{257,1},{2,258},{258,2},{3,259},{259,3},{4... | collective-permute-start | bytes 49160 | tf_op jit(solution)/shard_map/ppermute | solution.py:148
  42.6 28.8 %copy-start = (f32[512,1024]{1,0:T(8,128)S(1)}, f32[512,1024]{1,0:T(8,128)}, u32[]{:S(2)}) copy-start(f32[512,1024]{1,0:T(8,128)} %matrix.3) | copy-start | bytes 6291460
  119.4 29.2 %copy-start.1 = (f32[512,1024]{1,0:T(8,128)S(1)}, f32[512,1024]{1,0:T(8,128)}, u32[]{:S(2)}) copy-start(f32[512,1024]{1,0:T(8,128)} %matrix.3) | copy-start | bytes 6291460
  119.4 29.2 %copy-start.2 = (f32[2,128,128]{2,1,0:T(8,128)S(1)}, f32[2,128,128]{2,1,0:T(8,128)}, u32[]{:S(2)}) copy-start(f32[2,128,128]{2,1,0:T(8,128)} %factors.1) | copy-start | bytes 393220

commit v5 on v4

--- a/solution.py
+++ b/solution.py
@@ -51,20 +51,26 @@
     return jnp.concatenate(parts, axis=0)
 
 
-def part_kernel(odd, matrix, got, own, message):
+def part_kernel(odd, core, matrix, got, own, message):
     k = own.shape[-1] // 2
     v0 = in_order(got, 0, 16, odd[0])
     v1 = in_order(got, 16, 16, 1 - odd[0])
     part = product([matrix[:, :512], matrix[:, 512:]], [v0, v1], INNER)
-    message[:, 0:16] = part.reshape(32, 16, 2 * k)
+    slots = (core[0], 1 - core[0])
+    for chip in range(8):
+        for other in range(2):
+            piece = part[64 * chip + 32 * other : 64 * chip + 32 * other + 32].reshape(1, 2, 16, 2 * k)
+            message[pl.ds(slots[other], 1), 2 * chip : 2 * chip + 2, 0:16] = piece
     row = got[:, 32:48].reshape(512, 2 * k)
     gram = mm(row.T, part)
     cross = mm(own[:, :k].T, own[:, k:])
     low = jnp.concatenate([cross, gram[k:, k:]], axis=1)
     pieces = jnp.concatenate([gram[:k], low], axis=0).reshape(16, 2, 8, 2 * k)
+    flips = (odd[0] ^ core[0], 1 - (odd[0] ^ core[0]))
     for chip in range(8):
-        message[pl.ds(4 * chip + 2 * odd[0], 2), 16:24] = pieces[2 * chip]
-        message[pl.ds(4 * chip + 2 * (1 - odd[0]), 2), 16:24] = pieces[2 * chip + 1]
+        for ring in range(2):
+            piece = pieces[2 * chip + ring].reshape(1, 2, 8, 2 * k)
+            message[pl.ds(flips[ring], 1), 2 * chip : 2 * chip + 2, 16:24] = piece
 
 
 def update_kernel(odd, matrix, got_v, got_z, factors, out, held, sems):
@@ -103,8 +109,8 @@
 def part_of(*args):
     return pl.pallas_call(
         part_kernel,
-        out_shape=jax.ShapeDtypeStruct((32, 24, args[-1].shape[-1]), jnp.float32),
-        in_specs=[pl.BlockSpec(memory_space=pltpu.SMEM)] + [pl.BlockSpec(memory_space=pltpu.VMEM)] * 3,
+        out_shape=jax.ShapeDtypeStruct((2, 16, 24, args[-1].shape[-1]), jnp.float32),
+        in_specs=[pl.BlockSpec(memory_space=pltpu.SMEM)] * 2 + [pl.BlockSpec(memory_space=pltpu.VMEM)] * 3,
         out_specs=pl.BlockSpec(memory_space=pltpu.VMEM),
         compiler_params=pltpu.CompilerParams(vmem_limit_bytes=LIMIT),
     )(*args)
@@ -147,10 +153,14 @@
     halves = mine.reshape(2, 16, 2 * k)
     theirs = lax.ppermute(jnp.where(half == 0, halves[1], halves[0]), "x_lo", [(0, 1), (1, 0)])
     own_v = jnp.stack([jnp.where(half == 0, halves[0], theirs), jnp.where(half == 0, theirs, halves[1])])
-    odd, own_v = lax.optimization_barrier((odd, own_v))
+    core = lax.axis_index("core").reshape(1)
+    near = lax.axis_index("core") == 0
+    odd, core, near, own_v = lax.optimization_barrier((odd, core, near, own_v))
     got_v = spread(gather(own_v), own_v)
-    sums = exchange(part_of(odd, matrix, got_v, own_v.reshape(32, 2 * k)), PLANE)
-    sums = jnp.sum(sums.reshape(16, 2, 24, 2 * k), axis=0)
+    message = part_of(odd, core, matrix, got_v, own_v.reshape(32, 2 * k))
+    both = lax.all_gather(message[1], "core")
+    pair = message[0] + jnp.where(near, both[1], both[0])
+    sums = jnp.sum(exchange(pair, ("y", "x_hi", "x_lo")).reshape(8, 2, 24, 2 * k), axis=0)
     own_z = sums[:, :16]
     own_g = jnp.sum(sums[:, 16:], axis=0)
     gathered = gather(jnp.concatenate([own_z.reshape(32, 2 * k), own_g], axis=0))

time: 153 us -> 150 us (0.980)
  blocking collectives: 140 us -> 137 us
    all_to_all x3, blocking collectives: 76.4 us -> 69.6 us  [exchange(): return lax.all_to_all(parts, axes, 0, 0)]
    all_gather x0 -> x1, blocking collectives: none -> 3.34 us  [body(): both = lax.all_gather(message[1], 'core')]
where the time goes in v5:
time: 150 us; the launch traced here: 149 us
  blocking collectives  137 us (91%)
  Pallas kernels  5.51 us (4%)
  starting transfers between devices  3.94 us (3%)
    all_to_all x3, blocking collectives, exchange(): return lax.all_to_all(parts, axes, 0, 0)  69.6 us
    all_gather x2, blocking collectives, gather(): return lax.all_gather(piece, ('z', 'core'), axis_index_groups=RINGS)  64.1 us
    ppermute x1, starting transfers between devices, body(): lax.ppermute(jnp.where(half == 0, halves[1], halves[0]), 'x_lo', [(0, 1),...  3.94 us
    pallas_call x1, Pallas kernels, updated_of(): pl.pallas_call(update_kernel, out_shape=jax.ShapeDtypeStruct(shape, jnp.f...  3.81 us
    all_gather x1, blocking collectives, body(): both = lax.all_gather(message[1], 'core')  3.34 us
  transfers between devices with their start and end apart: 1, of which 1 were waited for; matrix products, arithmetic and copies ran while one was open for 0% of the time, Pallas kernels for 0%

profile of v5, /device:TPU:1, one launch (start us, length us, event | category | flops | bytes accessed | tf_op | source)
XLA Modules:
  0.0 149.4 jit_solution(7026391993771642086)
XLA Ops:
  0.0 0.7 slice_bitcast_fusion.1
  0.7 3.9 %collective-permute-start = (f32[16,256]{1,0:T(8,128)S(1)}, f32[16,256]{1,0:T(8,128)S(1)}, u32[]{:S(2)}, u32[]{:S(2)}) collective-permute-start(f32[16,256]{1,0:T(8,128)S(1)} %broadcast_select_fusion), channel_id=1, source_target_pairs={{0,256},{256,0},{1,257},{257,1},{2,258},{258,2},{3,259},{259,3},{4... | collective-permute-start | bytes 49160 | tf_op jit(solution)/shard_map/ppermute | solution.py:154
  4.7 1.1 collective-permute-done
  5.8 36.4 %all-gather = f32[32,16,256]{2,1,0:T(8,128)S(1)} all-gather(f32[2,16,256]{2,1,0:T(8,128)S(1)} %pad_maximum_fusion.3), channel_id=2, replica_groups={{0,17,32,49,64,81,96,113,128,145,160,177,192,209,224,241},{1,16,33,48,6..., dimensions={0}, use_global_device_ids=true | all-gather | bytes 557056 | tf_op jit(solution)/shard_map/all_gather | solution.py:136
  42.2 0.1 broadcast_in_dim.16
  42.3 0.1 broadcast_in_dim.15
  42.4 0.1 pad_maximum_fusion.1
  42.5 0.0 copy-start
  42.6 28.8 %all_to_all.15.got.got_v = f32[32,48,256]{2,1,0:T(8,128)S(1)} all-to-all(f32[32,48,256]{2,1,0:T(8,128)S(1)} %bitcast.28), channel_id=1, replica_groups=mesh['x_lo'=2,'z'=16,'y'=4,'x_hi'=2,'core'=2] {'y','x_hi','core','x_lo'}, dimensions={0} | all-to-all | bytes 3145728 | tf_op jit(solution)/shard_map/all_to_all | solution.py:132
  71.3 0.0 copy-done
  71.3 1.7 %shard_map.37 = f32[2,16,24,256]{3,2,1,0:T(8,128)S(1)} custom-call(s32[1]{0:T(128)} %bitcast.odd, s32[1]{0:T(128)} %bitcast.1.core, f32[512,1024]{1,0:T(8,128)S(1)} %copy-done, f32[32,48,256]{2,1,0:T(8,128)S(1)} %all_to_all.15.got.got_v, f32[32,256]{1,0:T(8,128)S(1)} %bitcast.26), custom_call_target="tpu_custom_call" | custom-call | tf_op jit(solution)/shard_map/pallas_call | solution.py:110
  73.0 3.3 %all_gather.17 = f32[2,16,24,256]{3,2,1,0:T(8,128)S(1)} all-gather(f32[1,16,24,256]{3,2,1,0:T(8,128)S(1)} %slice.55), channel_id=1, replica_groups=mesh['x_lo'=2,'z'=16,'y'=4,'x_hi'=2,'core'=2] {'core'}, dimensions={0}, use_global_device_ids=true | all-gather | bytes 1179648 | tf_op jit(solution)/shard_map/all_gather | solution.py:161
  76.4 0.1 fusion.1
  76.5 13.1 %all_to_all.16 = f32[16,24,256]{2,1,0:T(8,128)S(1)} all-to-all(f32[16,24,256]{2,1,0:T(8,128)S(1)} %fusion.1), channel_id=1, replica_groups=mesh['x_lo'=2,'z'=16,'y'=4,'x_hi'=2,'core'=2] {'y','x_hi','x_lo'}, dimensions={0} | all-to-all | bytes 786432 | tf_op jit(solution)/shard_map/all_to_all | solution.py:132
  89.6 27.7 %all-gather.1 = f32[640,256]{1,0:T(8,128)S(1)} all-gather(f32[40,256]{1,0:T(8,128)S(1)} %pad_maximum_fusion.2), channel_id=3, replica_groups={{0,17,32,49,64,81,96,113,128,145,160,177,192,209,224,241},{1,16,33,48,6..., dimensions={0}, use_global_device_ids=true | all-gather | bytes 696320 | tf_op jit(solution)/shard_map/all_gather | solution.py:136
  117.5 0.1 broadcast_in_dim.36
  117.5 0.1 broadcast_in_dim.35
  117.7 0.2 pad_maximum_fusion
  117.8 0.0 copy-start.1
  117.9 0.0 copy-start.2
  117.9 27.7 %all_to_all.17.got_z = f32[32,56,256]{2,1,0:T(8,128)S(1)} all-to-all(f32[32,56,256]{2,1,0:T(8,128)S(1)} %bitcast.27), channel_id=1, replica_groups=mesh['x_lo'=2,'z'=16,'y'=4,'x_hi'=2,'core'=2] {'y','x_hi','core','x_lo'}, dimensions={0} | all-to-all | bytes 3670016 | tf_op jit(solution)/shard_map/all_to_all | solution.py:132
  145.6 0.0 copy-done.1
  145.6 0.0 copy-done.2
  145.6 3.8 %shard_map.38 = f32[512,1024]{1,0:T(8,128)} custom-call(s32[1]{0:T(128)} %bitcast.odd, f32[512,1024]{1,0:T(8,128)S(1)} %copy-done.1, f32[32,48,256]{2,1,0:T(8,128)S(1)} %all_to_all.15.got.got_v, f32[32,56,256]{2,1,0:T(8,128)S(1)} %all_to_all.17.got_z, f32[2,128,128]{2,1,0:T(8,128)S(1)} %copy-done.2), custom_call_target="tpu_custom_call" | custom-call | tf_op jit(solution)/shard_map/pallas_call | solution.py:121
  (13 shorter events, 0.2 us)
Async XLA Ops:
  0.7 5.1 %collective-permute-start = (f32[16,256]{1,0:T(8,128)S(1)}, f32[16,256]{1,0:T(8,128)S(1)}, u32[]{:S(2)}, u32[]{:S(2)}) collective-permute-start(f32[16,256]{1,0:T(8,128)S(1)} %broadcast_select_fusion), channel_id=1, source_target_pairs={{0,256},{256,0},{1,257},{257,1},{2,258},{258,2},{3,259},{259,3},{4... | collective-permute-start | bytes 49160 | tf_op jit(solution)/shard_map/ppermute | solution.py:154
  42.5 28.8 %copy-start = (f32[512,1024]{1,0:T(8,128)S(1)}, f32[512,1024]{1,0:T(8,128)}, u32[]{:S(2)}) copy-start(f32[512,1024]{1,0:T(8,128)} %matrix.3) | copy-start | bytes 6291460
  117.8 27.8 %copy-start.1 = (f32[512,1024]{1,0:T(8,128)S(1)}, f32[512,1024]{1,0:T(8,128)}, u32[]{:S(2)}) copy-start(f32[512,1024]{1,0:T(8,128)} %matrix.3) | copy-start | bytes 6291460
  117.9 27.7 %copy-start.2 = (f32[2,128,128]{2,1,0:T(8,128)S(1)}, f32[2,128,128]{2,1,0:T(8,128)}, u32[]{:S(2)}) copy-start(f32[2,128,128]{2,1,0:T(8,128)} %factors.1) | copy-start | bytes 393220

commit v6 on v5

--- a/solution.py
+++ b/solution.py
@@ -147,12 +147,11 @@
 
 def body(matrix, vectors, factors):
     k = vectors.shape[-1]
-    mine = jnp.concatenate([vectors[0], vectors[1]], axis=1)
     odd = (lax.axis_index("z") & 1).reshape(1)
-    half = lax.axis_index("x_lo")
-    halves = mine.reshape(2, 16, 2 * k)
-    theirs = lax.ppermute(jnp.where(half == 0, halves[1], halves[0]), "x_lo", [(0, 1), (1, 0)])
-    own_v = jnp.stack([jnp.where(half == 0, halves[0], theirs), jnp.where(half == 0, theirs, halves[1])])
+    left = lax.axis_index("x_lo") == 0
+    pair = lax.all_gather(vectors, "x_lo")
+    half = jnp.where(left, pair[:, :, :16], pair[:, :, 16:])
+    own_v = jnp.concatenate([half[:, 0], half[:, 1]], axis=-1)
     core = lax.axis_index("core").reshape(1)
     near = lax.axis_index("core") == 0
     odd, core, near, own_v = lax.optimization_barrier((odd, core, near, own_v))

time: 150 us -> 148 us (0.987)
  blocking collectives: 137 us -> 141 us
  starting transfers between devices: 3.94 us -> 0 us
    all_gather x0 -> x1, blocking collectives: none -> 4.26 us  [body(): pair = lax.all_gather(vectors, 'x_lo')]
    ppermute x1 -> x0, starting transfers between devices: 3.94 us -> none  [body(): lax.ppermute(jnp.where(half == 0, halves[1], halves[0]), 'x_lo', [(0, 1),...]
  transfers between devices with their start and end apart: 1 -> 0, of which waited for: 1 -> 0; matrix products, arithmetic and copies ran while one was open for 0% -> 0% of each run, Pallas kernels for 0% -> 0%
where the time goes in v6:
time: 148 us
  blocking collectives  141 us (95%)
  Pallas kernels  5.51 us (4%)
    all_to_all x3, blocking collectives, exchange(): return lax.all_to_all(parts, axes, 0, 0)  69.5 us
    all_gather x2, blocking collectives, gather(): return lax.all_gather(piece, ('z', 'core'), axis_index_groups=RINGS)  64.2 us
    all_gather x1, blocking collectives, body(): pair = lax.all_gather(vectors, 'x_lo')  4.26 us
    pallas_call x1, Pallas kernels, updated_of(): pl.pallas_call(update_kernel, out_shape=jax.ShapeDtypeStruct(shape, jnp.f...  3.81 us
    all_gather x1, blocking collectives, body(): both = lax.all_gather(message[1], 'core')  3.35 us

profile of v6, /device:TPU:1, one launch (start us, length us, event | category | flops | bytes accessed | tf_op | source)
XLA Modules:
  0.0 148.0 jit_solution(10245957975056892185)
XLA Ops:
  0.0 4.3 %all-gather = f32[4,32,128]{2,1,0:T(8,128)S(1)} all-gather(f32[2,32,128]{2,1,0:T(8,128)} %param.4), channel_id=2, replica_groups=mesh['x_lo'=2,'z'=16,'y'=4,'x_hi'=2,'core'=2] {'x_lo'}, dimensions={0}, use_global_device_ids=true | all-gather | bytes 98304 | tf_op jit(solution)/shard_map/all_gather | solution.py:152
  4.3 36.4 %all-gather.1 = f32[32,16,256]{2,1,0:T(8,128)S(1)} all-gather(f32[2,16,256]{2,1,0:T(8,128)S(1)} %pad_maximum_fusion.3), channel_id=3, replica_groups={{0,17,32,49,64,81,96,113,128,145,160,177,192,209,224,241},{1,16,33,48,6..., dimensions={0}, use_global_device_ids=true | all-gather | bytes 557056 | tf_op jit(solution)/shard_map/all_gather | solution.py:136
  40.7 0.1 broadcast_in_dim.16
  40.8 0.1 broadcast_in_dim.15
  40.9 0.1 pad_maximum_fusion.1
  41.0 0.0 copy-start
  41.0 28.8 %all_to_all.15.got.got_v = f32[32,48,256]{2,1,0:T(8,128)S(1)} all-to-all(f32[32,48,256]{2,1,0:T(8,128)S(1)} %bitcast.25), channel_id=1, replica_groups=mesh['x_lo'=2,'z'=16,'y'=4,'x_hi'=2,'core'=2] {'y','x_hi','core','x_lo'}, dimensions={0} | all-to-all | bytes 3145728 | tf_op jit(solution)/shard_map/all_to_all | solution.py:132
  69.8 0.0 copy-done
  69.8 1.7 %shard_map.37 = f32[2,16,24,256]{3,2,1,0:T(8,128)S(1)} custom-call(s32[1]{0:T(128)} %bitcast.odd, s32[1]{0:T(128)} %bitcast.1.core, f32[512,1024]{1,0:T(8,128)S(1)} %copy-done, f32[32,48,256]{2,1,0:T(8,128)S(1)} %all_to_all.15.got.got_v, f32[32,256]{1,0:T(8,128)S(1)} %bitcast.23), custom_call_target="tpu_custom_call" | custom-call | tf_op jit(solution)/shard_map/pallas_call | solution.py:110
  71.5 3.4 %all_gather.25 = f32[2,16,24,256]{3,2,1,0:T(8,128)S(1)} all-gather(f32[1,16,24,256]{3,2,1,0:T(8,128)S(1)} %slice.53), channel_id=1, replica_groups=mesh['x_lo'=2,'z'=16,'y'=4,'x_hi'=2,'core'=2] {'core'}, dimensions={0}, use_global_device_ids=true | all-gather | bytes 1179648 | tf_op jit(solution)/shard_map/all_gather | solution.py:160
  74.9 0.1 fusion.1
  74.9 13.1 %all_to_all.16 = f32[16,24,256]{2,1,0:T(8,128)S(1)} all-to-all(f32[16,24,256]{2,1,0:T(8,128)S(1)} %fusion.1), channel_id=1, replica_groups=mesh['x_lo'=2,'z'=16,'y'=4,'x_hi'=2,'core'=2] {'y','x_hi','x_lo'}, dimensions={0} | all-to-all | bytes 786432 | tf_op jit(solution)/shard_map/all_to_all | solution.py:132
  88.0 27.9 %all-gather.2 = f32[640,256]{1,0:T(8,128)S(1)} all-gather(f32[40,256]{1,0:T(8,128)S(1)} %pad_maximum_fusion.2), channel_id=4, replica_groups={{0,17,32,49,64,81,96,113,128,145,160,177,192,209,224,241},{1,16,33,48,6..., dimensions={0}, use_global_device_ids=true | all-gather | bytes 696320 | tf_op jit(solution)/shard_map/all_gather | solution.py:136
  116.1 0.1 broadcast_in_dim.36
  116.2 0.1 broadcast_in_dim.35
  116.3 0.2 pad_maximum_fusion
  116.5 0.0 copy-start.1
  116.5 0.0 copy-start.2
  116.5 27.7 %all_to_all.17.got_z = f32[32,56,256]{2,1,0:T(8,128)S(1)} all-to-all(f32[32,56,256]{2,1,0:T(8,128)S(1)} %bitcast.24), channel_id=1, replica_groups=mesh['x_lo'=2,'z'=16,'y'=4,'x_hi'=2,'core'=2] {'y','x_hi','core','x_lo'}, dimensions={0} | all-to-all | bytes 3670016 | tf_op jit(solution)/shard_map/all_to_all | solution.py:132
  144.2 0.0 copy-done.1
  144.2 0.0 copy-done.2
  144.2 3.8 %shard_map.38 = f32[512,1024]{1,0:T(8,128)} custom-call(s32[1]{0:T(128)} %bitcast.odd, f32[512,1024]{1,0:T(8,128)S(1)} %copy-done.1, f32[32,48,256]{2,1,0:T(8,128)S(1)} %all_to_all.15.got.got_v, f32[32,56,256]{2,1,0:T(8,128)S(1)} %all_to_all.17.got_z, f32[2,128,128]{2,1,0:T(8,128)S(1)} %copy-done.2), custom_call_target="tpu_custom_call" | custom-call | tf_op jit(solution)/shard_map/pallas_call | solution.py:121
  (14 shorter events, 0.3 us)
Async XLA Ops:
  41.0 28.8 %copy-start = (f32[512,1024]{1,0:T(8,128)S(1)}, f32[512,1024]{1,0:T(8,128)}, u32[]{:S(2)}) copy-start(f32[512,1024]{1,0:T(8,128)} %matrix.3) | copy-start | bytes 6291460
  116.5 27.7 %copy-start.1 = (f32[512,1024]{1,0:T(8,128)S(1)}, f32[512,1024]{1,0:T(8,128)}, u32[]{:S(2)}) copy-start(f32[512,1024]{1,0:T(8,128)} %matrix.3) | copy-start | bytes 6291460
  116.5 27.7 %copy-start.2 = (f32[2,128,128]{2,1,0:T(8,128)S(1)}, f32[2,128,128]{2,1,0:T(8,128)}, u32[]{:S(2)}) copy-start(f32[2,128,128]{2,1,0:T(8,128)} %factors.1) | copy-start | bytes 393220

commit v7 on v6

--- a/solution.py
+++ b/solution.py
@@ -73,10 +73,10 @@
             message[pl.ds(flips[ring], 1), 2 * chip : 2 * chip + 2, 16:24] = piece
 
 
-def update_kernel(odd, matrix, got_v, got_z, factors, out, held, sems):
+def update_kernel(odd, matrix, got_v, got_z, halves, factors, out, held, sems):
     k = factors.shape[-1]
     f1, f2 = factors[0], factors[1]
-    gram = in_order(got_z, 48, 8, odd[0])
+    gram = in_order(got_z, 40, 8, odd[0])
     g11, g12, h12, g22 = gram[:k, :k], gram[:k, k:], gram[k:, :k], gram[k:, k:]
     p12 = -mm(mm(f1, h12), f2)
     p = jnp.concatenate(
@@ -85,7 +85,8 @@
     full = jnp.concatenate([gram[:k], jnp.concatenate([g12.T, g22], axis=1)], axis=0)
     gp = mm(full, p)
     on_z = product([got_v[:, 32:48].reshape(512, 2 * k)], [p], LAST)
-    on_v = product([got_z[:, 32:48].reshape(512, 2 * k), on_z], [p, -gp], INNER)
+    z_row = jnp.concatenate([halves[0], halves[1]], axis=1).reshape(512, 2 * k)
+    on_v = product([z_row, on_z], [p, -gp], INNER)
     left = thrice([on_z, on_v])
     chips = 16 // CHUNKS
     wide = 64 * chips
@@ -121,7 +122,7 @@
     return pl.pallas_call(
         update_kernel,
         out_shape=jax.ShapeDtypeStruct(shape, jnp.float32),
-        in_specs=[pl.BlockSpec(memory_space=pltpu.SMEM)] + [pl.BlockSpec(memory_space=pltpu.VMEM)] * 4,
+        in_specs=[pl.BlockSpec(memory_space=pltpu.SMEM)] + [pl.BlockSpec(memory_space=pltpu.VMEM)] * 5,
         out_specs=pl.BlockSpec(memory_space=pl.ANY),
         scratch_shapes=[pltpu.VMEM(shape, jnp.float32), pltpu.SemaphoreType.DMA((CHUNKS,))],
         compiler_params=pltpu.CompilerParams(vmem_limit_bytes=LIMIT),
@@ -140,7 +141,7 @@
     width = stack.shape[-1]
     cols = stack.reshape(8, 2, 2, 16, width).transpose(2, 0, 1, 3, 4).reshape(16, 1, 32, width)
     pieces = [jnp.broadcast_to(cols, (16, 2, 32, width))]
-    pieces += [jnp.broadcast_to(c[None], (16, 2) + c.shape[1:]) for c in common]
+    pieces += [jnp.broadcast_to(c, (8, 2, 2) + c.shape[2:]).reshape((16, 2) + c.shape[2:]) for c in common]
     message = jnp.concatenate(pieces, axis=2)
     return exchange(message.reshape((32,) + message.shape[2:]), PLANE)
 
@@ -155,7 +156,7 @@
     core = lax.axis_index("core").reshape(1)
     near = lax.axis_index("core") == 0
     odd, core, near, own_v = lax.optimization_barrier((odd, core, near, own_v))
-    got_v = spread(gather(own_v), own_v)
+    got_v = spread(gather(own_v), own_v[None])
     message = part_of(odd, core, matrix, got_v, own_v.reshape(32, 2 * k))
     both = lax.all_gather(message[1], "core")
     pair = message[0] + jnp.where(near, both[1], both[0])
@@ -163,8 +164,11 @@
     own_z = sums[:, :16]
     own_g = jnp.sum(sums[:, 16:], axis=0)
     gathered = gather(jnp.concatenate([own_z.reshape(32, 2 * k), own_g], axis=0))
-    got_z = spread(gathered[:, :32].reshape(16, 2, 16, 2 * k), own_z, jnp.sum(gathered[:, 32:], axis=0)[None])
-    return updated_of(odd, matrix, got_v, got_z, factors)
+    split_z = own_z.reshape(2, 2, 8, 2 * k).transpose(1, 0, 2, 3)
+    total_g = jnp.sum(gathered[:, 32:], axis=0)[None, None]
+    got_z = spread(gathered[:, :32].reshape(16, 2, 16, 2 * k), split_z, total_g)
+    halves = lax.all_gather(got_z[:, 32:40], "core")
+    return updated_of(odd, matrix, got_v, got_z, halves, factors)
 
 
 def solution(mesh):

time: 148 us -> 149 us (level)
    all_gather x0 -> x1, blocking collectives: none -> 3.15 us  [body(): halves = lax.all_gather(got_z[:, 32:40], 'core')]
    all_to_all x3, blocking collectives: 69.5 us -> 66.7 us  [exchange(): return lax.all_to_all(parts, axes, 0, 0)]
where the time goes in v7:
time: 149 us; the launch traced here: 148 us
  blocking collectives  142 us (95%)
  Pallas kernels  5.52 us (4%)
    all_to_all x3, blocking collectives, exchange(): return lax.all_to_all(parts, axes, 0, 0)  66.7 us
    all_gather x2, blocking collectives, gather(): return lax.all_gather(piece, ('z', 'core'), axis_index_groups=RINGS)  64.2 us
    all_gather x1, blocking collectives, body(): pair = lax.all_gather(vectors, 'x_lo')  4.26 us
    pallas_call x1, Pallas kernels, updated_of(): pl.pallas_call(update_kernel, out_shape=jax.ShapeDtypeStruct(shape, jnp.f...  3.82 us
    all_gather x1, blocking collectives, body(): both = lax.all_gather(message[1], 'core')  3.35 us
    all_gather x1, blocking collectives, body(): halves = lax.all_gather(got_z[:, 32:40], 'core')  3.15 us

profile of v7, /device:TPU:1, one launch (start us, length us, event | category | flops | bytes accessed | tf_op | source)
XLA Modules:
  0.0 148.3 jit_solution(5934264930027477079)
XLA Ops:
  0.0 4.3 %all-gather = f32[4,32,128]{2,1,0:T(8,128)S(1)} all-gather(f32[2,32,128]{2,1,0:T(8,128)} %param.4), channel_id=2, replica_groups=mesh['x_lo'=2,'z'=16,'y'=4,'x_hi'=2,'core'=2] {'x_lo'}, dimensions={0}, use_global_device_ids=true | all-gather | bytes 98304 | tf_op jit(solution)/shard_map/all_gather | solution.py:153
  4.3 36.4 %all-gather.1 = f32[32,16,256]{2,1,0:T(8,128)S(1)} all-gather(f32[2,16,256]{2,1,0:T(8,128)S(1)} %pad_maximum_fusion.3), channel_id=3, replica_groups={{0,17,32,49,64,81,96,113,128,145,160,177,192,209,224,241},{1,16,33,48,6..., dimensions={0}, use_global_device_ids=true | all-gather | bytes 557056 | tf_op jit(solution)/shard_map/all_gather | solution.py:137
  40.7 0.1 reshape.46
  40.8 0.1 broadcast_in_dim.11
  40.9 0.1 pad_maximum_fusion
  41.0 0.0 copy-start
  41.0 28.8 %all_to_all.15.got.got_v = f32[32,48,256]{2,1,0:T(8,128)S(1)} all-to-all(f32[32,48,256]{2,1,0:T(8,128)S(1)} %bitcast.31), channel_id=1, replica_groups=mesh['x_lo'=2,'z'=16,'y'=4,'x_hi'=2,'core'=2] {'y','x_hi','core','x_lo'}, dimensions={0} | all-to-all | bytes 3145728 | tf_op jit(solution)/shard_map/all_to_all | solution.py:133
  69.8 0.0 copy-done
  69.8 1.7 %shard_map.37 = f32[2,16,24,256]{3,2,1,0:T(8,128)S(1)} custom-call(s32[1]{0:T(128)} %bitcast.odd, s32[1]{0:T(128)} %bitcast.1.core, f32[512,1024]{1,0:T(8,128)S(1)} %copy-done, f32[32,48,256]{2,1,0:T(8,128)S(1)} %all_to_all.15.got.got_v, f32[32,256]{1,0:T(8,128)S(1)} %bitcast.30), custom_call_target="tpu_custom_call" | custom-call | tf_op jit(solution)/shard_map/pallas_call | solution.py:111
  71.5 3.4 %all_gather.31 = f32[2,16,24,256]{3,2,1,0:T(8,128)S(1)} all-gather(f32[1,16,24,256]{3,2,1,0:T(8,128)S(1)} %slice.57), channel_id=1, replica_groups=mesh['x_lo'=2,'z'=16,'y'=4,'x_hi'=2,'core'=2] {'core'}, dimensions={0}, use_global_device_ids=true | all-gather | bytes 1179648 | tf_op jit(solution)/shard_map/all_gather | solution.py:161
  74.9 0.1 fusion.1
  74.9 13.1 %all_to_all.16 = f32[16,24,256]{2,1,0:T(8,128)S(1)} all-to-all(f32[16,24,256]{2,1,0:T(8,128)S(1)} %fusion.1), channel_id=1, replica_groups=mesh['x_lo'=2,'z'=16,'y'=4,'x_hi'=2,'core'=2] {'y','x_hi','x_lo'}, dimensions={0} | all-to-all | bytes 786432 | tf_op jit(solution)/shard_map/all_to_all | solution.py:133
  88.1 27.9 %all-gather.2 = f32[640,256]{1,0:T(8,128)S(1)} all-gather(f32[40,256]{1,0:T(8,128)S(1)} %pad_maximum_fusion.2), channel_id=4, replica_groups={{0,17,32,49,64,81,96,113,128,145,160,177,192,209,224,241},{1,16,33,48,6..., dimensions={0}, use_global_device_ids=true | all-gather | bytes 696320 | tf_op jit(solution)/shard_map/all_gather | solution.py:137
  116.1 0.1 broadcast_in_dim.13
  116.3 0.2 pad_maximum_fusion.1
  116.4 0.0 copy-start.1
  116.4 0.0 copy-start.2
  116.4 24.9 %all_to_all.17.got_z = f32[32,48,256]{2,1,0:T(8,128)S(1)} all-to-all(f32[32,48,256]{2,1,0:T(8,128)S(1)} %pad_maximum_fusion.1), channel_id=1, replica_groups=mesh['x_lo'=2,'z'=16,'y'=4,'x_hi'=2,'core'=2] {'y','x_hi','core','x_lo'}, dimensions={0} | all-to-all | bytes 3145728 | tf_op jit(solution)/shard_map/all_to_all | solution.py:133
  141.3 3.2 %all-gather.3 = f32[64,8,256]{2,1,0:T(8,128)S(1)} all-gather(f32[32,8,256]{2,1,0:T(8,128)S(1)} %slice.64), channel_id=5, replica_groups=mesh['x_lo'=2,'z'=16,'y'=4,'x_hi'=2,'core'=2] {'core'}, dimensions={0}, use_global_device_ids=true | all-gather | bytes 786432 | tf_op jit(solution)/shard_map/all_gather | solution.py:170
  144.5 0.0 copy-done.1
  144.5 0.0 copy-done.2
  144.5 3.8 %shard_map.38 = f32[512,1024]{1,0:T(8,128)} custom-call(s32[1]{0:T(128)} %bitcast.odd, f32[512,1024]{1,0:T(8,128)S(1)} %copy-done.1, f32[32,48,256]{2,1,0:T(8,128)S(1)} %all_to_all.15.got.got_v, f32[32,48,256]{2,1,0:T(8,128)S(1)} %all_to_all.17.got_z, f32[2,32,8,256]{3,2,1,0:T(8,128)S(1)} %bitcast.29, f32[2,128,128]{2,1,0:T(8,128)S(1)} %copy-done.2), custom_call_target="tpu_custom_call" | custom-call | tf_op jit(solution)/shard_map/pallas_call | solution.py:122
  (17 shorter events, 0.3 us)
Async XLA Ops:
  41.0 28.8 %copy-start = (f32[512,1024]{1,0:T(8,128)S(1)}, f32[512,1024]{1,0:T(8,128)}, u32[]{:S(2)}) copy-start(f32[512,1024]{1,0:T(8,128)} %matrix.3) | copy-start | bytes 6291460
  116.4 28.1 %copy-start.1 = (f32[512,1024]{1,0:T(8,128)S(1)}, f32[512,1024]{1,0:T(8,128)}, u32[]{:S(2)}) copy-start(f32[512,1024]{1,0:T(8,128)} %matrix.3) | copy-start | bytes 6291460
  116.4 28.1 %copy-start.2 = (f32[2,128,128]{2,1,0:T(8,128)S(1)}, f32[2,128,128]{2,1,0:T(8,128)}, u32[]{:S(2)}) copy-start(f32[2,128,128]{2,1,0:T(8,128)} %factors.1) | copy-start | bytes 393220

commit v8 on v6

--- a/solution.py
+++ b/solution.py
@@ -42,6 +42,16 @@
     return product([left], [right], INNER)
 
 
+def over_rows(left, right):
+    left, right = split(left), split(right)
+    return lax.dot_general(
+        jnp.concatenate([left[0], left[1], left[0]], axis=0),
+        jnp.concatenate([right[0], right[0], right[1]], axis=0),
+        (((0,), (0,)), ((), ())),
+        preferred_element_type=jnp.float32,
+    )
+
+
 def in_order(got, first, size, swap, chip_from=0, chips=8):
     parts = []
     for chip in range(chip_from, chip_from + chips):
@@ -62,8 +72,8 @@
             piece = part[64 * chip + 32 * other : 64 * chip + 32 * other + 32].reshape(1, 2, 16, 2 * k)
             message[pl.ds(slots[other], 1), 2 * chip : 2 * chip + 2, 0:16] = piece
     row = got[:, 32:48].reshape(512, 2 * k)
-    gram = mm(row.T, part)
-    cross = mm(own[:, :k].T, own[:, k:])
+    gram = over_rows(row, part)
+    cross = over_rows(own[:, :k], own[:, k:])
     low = jnp.concatenate([cross, gram[k:, k:]], axis=1)
     pieces = jnp.concatenate([gram[:k], low], axis=0).reshape(16, 2, 8, 2 * k)
     flips = (odd[0] ^ core[0], 1 - (odd[0] ^ core[0]))

time: 148 us -> 148 us (level)
  no operation moved by 1% of the time
where the time goes in v8:
time: 148 us
  blocking collectives  141 us (95%)
  Pallas kernels  5.51 us (4%)
    all_to_all x3, blocking collectives, exchange(): return lax.all_to_all(parts, axes, 0, 0)  69.5 us
    all_gather x2, blocking collectives, gather(): return lax.all_gather(piece, ('z', 'core'), axis_index_groups=RINGS)  64.3 us
    all_gather x1, blocking collectives, body(): pair = lax.all_gather(vectors, 'x_lo')  4.26 us
    pallas_call x1, Pallas kernels, updated_of(): pl.pallas_call(update_kernel, out_shape=jax.ShapeDtypeStruct(shape, jnp.f...  3.81 us
    all_gather x1, blocking collectives, body(): both = lax.all_gather(message[1], 'core')  3.35 us

profile of v8, /device:TPU:1, one launch (start us, length us, event | category | flops | bytes accessed | tf_op | source)
XLA Modules:
  0.0 148.0 jit_solution(10444310427865203958)
XLA Ops:
  0.0 4.3 %all-gather = f32[4,32,128]{2,1,0:T(8,128)S(1)} all-gather(f32[2,32,128]{2,1,0:T(8,128)} %param.4), channel_id=2, replica_groups=mesh['x_lo'=2,'z'=16,'y'=4,'x_hi'=2,'core'=2] {'x_lo'}, dimensions={0}, use_global_device_ids=true | all-gather | bytes 98304 | tf_op jit(solution)/shard_map/all_gather | solution.py:162
  4.3 36.4 %all-gather.1 = f32[32,16,256]{2,1,0:T(8,128)S(1)} all-gather(f32[2,16,256]{2,1,0:T(8,128)S(1)} %pad_maximum_fusion.3), channel_id=3, replica_groups={{0,17,32,49,64,81,96,113,128,145,160,177,192,209,224,241},{1,16,33,48,6..., dimensions={0}, use_global_device_ids=true | all-gather | bytes 557056 | tf_op jit(solution)/shard_map/all_gather | solution.py:146
  40.7 0.1 broadcast_in_dim.16
  40.8 0.1 broadcast_in_dim.15
  40.9 0.1 pad_maximum_fusion.1
  41.0 0.0 copy-start
  41.0 28.8 %all_to_all.15.got.got_v = f32[32,48,256]{2,1,0:T(8,128)S(1)} all-to-all(f32[32,48,256]{2,1,0:T(8,128)S(1)} %bitcast.25), channel_id=1, replica_groups=mesh['x_lo'=2,'z'=16,'y'=4,'x_hi'=2,'core'=2] {'y','x_hi','core','x_lo'}, dimensions={0} | all-to-all | bytes 3145728 | tf_op jit(solution)/shard_map/all_to_all | solution.py:142
  69.8 0.0 copy-done
  69.8 1.7 %shard_map.37 = f32[2,16,24,256]{3,2,1,0:T(8,128)S(1)} custom-call(s32[1]{0:T(128)} %bitcast.odd, s32[1]{0:T(128)} %bitcast.1.core, f32[512,1024]{1,0:T(8,128)S(1)} %copy-done, f32[32,48,256]{2,1,0:T(8,128)S(1)} %all_to_all.15.got.got_v, f32[32,256]{1,0:T(8,128)S(1)} %bitcast.23), custom_call_target="tpu_custom_call" | custom-call | tf_op jit(solution)/shard_map/pallas_call | solution.py:120
  71.5 3.4 %all_gather.25 = f32[2,16,24,256]{3,2,1,0:T(8,128)S(1)} all-gather(f32[1,16,24,256]{3,2,1,0:T(8,128)S(1)} %slice.53), channel_id=1, replica_groups=mesh['x_lo'=2,'z'=16,'y'=4,'x_hi'=2,'core'=2] {'core'}, dimensions={0}, use_global_device_ids=true | all-gather | bytes 1179648 | tf_op jit(solution)/shard_map/all_gather | solution.py:170
  74.9 0.1 fusion.1
  74.9 13.1 %all_to_all.16 = f32[16,24,256]{2,1,0:T(8,128)S(1)} all-to-all(f32[16,24,256]{2,1,0:T(8,128)S(1)} %fusion.1), channel_id=1, replica_groups=mesh['x_lo'=2,'z'=16,'y'=4,'x_hi'=2,'core'=2] {'y','x_hi','x_lo'}, dimensions={0} | all-to-all | bytes 786432 | tf_op jit(solution)/shard_map/all_to_all | solution.py:142
  88.1 27.9 %all-gather.2 = f32[640,256]{1,0:T(8,128)S(1)} all-gather(f32[40,256]{1,0:T(8,128)S(1)} %pad_maximum_fusion.2), channel_id=4, replica_groups={{0,17,32,49,64,81,96,113,128,145,160,177,192,209,224,241},{1,16,33,48,6..., dimensions={0}, use_global_device_ids=true | all-gather | bytes 696320 | tf_op jit(solution)/shard_map/all_gather | solution.py:146
  116.1 0.1 broadcast_in_dim.36
  116.2 0.1 broadcast_in_dim.35
  116.3 0.2 pad_maximum_fusion
  116.5 0.0 copy-start.1
  116.5 0.0 copy-start.2
  116.5 27.7 %all_to_all.17.got_z = f32[32,56,256]{2,1,0:T(8,128)S(1)} all-to-all(f32[32,56,256]{2,1,0:T(8,128)S(1)} %bitcast.24), channel_id=1, replica_groups=mesh['x_lo'=2,'z'=16,'y'=4,'x_hi'=2,'core'=2] {'y','x_hi','core','x_lo'}, dimensions={0} | all-to-all | bytes 3670016 | tf_op jit(solution)/shard_map/all_to_all | solution.py:142
  144.2 0.0 copy-done.1
  144.2 0.0 copy-done.2
  144.2 3.8 %shard_map.38 = f32[512,1024]{1,0:T(8,128)} custom-call(s32[1]{0:T(128)} %bitcast.odd, f32[512,1024]{1,0:T(8,128)S(1)} %copy-done.1, f32[32,48,256]{2,1,0:T(8,128)S(1)} %all_to_all.15.got.got_v, f32[32,56,256]{2,1,0:T(8,128)S(1)} %all_to_all.17.got_z, f32[2,128,128]{2,1,0:T(8,128)S(1)} %copy-done.2), custom_call_target="tpu_custom_call" | custom-call | tf_op jit(solution)/shard_map/pallas_call | solution.py:131
  (14 shorter events, 0.3 us)
Async XLA Ops:
  41.0 28.8 %copy-start = (f32[512,1024]{1,0:T(8,128)S(1)}, f32[512,1024]{1,0:T(8,128)}, u32[]{:S(2)}) copy-start(f32[512,1024]{1,0:T(8,128)} %matrix.3) | copy-start | bytes 6291460
  116.5 27.7 %copy-start.1 = (f32[512,1024]{1,0:T(8,128)S(1)}, f32[512,1024]{1,0:T(8,128)}, u32[]{:S(2)}) copy-start(f32[512,1024]{1,0:T(8,128)} %matrix.3) | copy-start | bytes 6291460
  116.5 27.7 %copy-start.2 = (f32[2,128,128]{2,1,0:T(8,128)S(1)}, f32[2,128,128]{2,1,0:T(8,128)}, u32[]{:S(2)}) copy-start(f32[2,128,128]{2,1,0:T(8,128)} %factors.1) | copy-start | bytes 393220
